TPU v7x, 128 devices: a whole 4x4x4 slice. The times are simulated.
128 devices in a mesh: ctx: 16 (over x, y), fsdp: 8 (over z, core).
Axes of the slice: x: 4, y: 4, z: 4, core: 2. Of those that a mesh axis runs over, the one named last changes fastest.
Arguments:
- hidden: bfloat16 [16, 8, 128, 960], P('ctx', 'fsdp'), may hold values from -6 to 6
- cotangent: bfloat16 [16, 8, 128, 960], P('ctx', 'fsdp'), may hold values from -6 to 6
- pairing: int32 [16], replicated, may hold values from 0 to 15, as said below
- documents: int32 [16, 8, 128], P(None, 'fsdp'), may hold values from 0 to 3, as said below
- attn_gain: bfloat16 [960], P('fsdp'), may hold values from 0.5 to 1.5
- w_query: bfloat16 [960, 960], P('fsdp'), may hold values from -0.1875 to 0.1875
- w_key: bfloat16 [960, 320], P('fsdp'), may hold values from -0.1875 to 0.1875
- w_value: bfloat16 [960, 320], P('fsdp'), may hold values from -0.1875 to 0.1875
- w_out: bfloat16 [960, 960], P('fsdp'), may hold values from -3 to 3
- mlp_gain: bfloat16 [960], P('fsdp'), may hold values from 0.5 to 1.5
- w_gate: bfloat16 [960, 2560], P('fsdp'), may hold values from -0.1875 to 0.1875
- w_up: bfloat16 [960, 2560], P('fsdp'), may hold values from -0.1875 to 0.1875
- w_down: bfloat16 [2560, 960], P('fsdp'), may hold values from -0.125 to 0.125
Outputs:
- result: bfloat16 [16, 8, 128, 960], P('ctx', 'fsdp')
- input_grad: bfloat16 [16, 8, 128, 960], P('ctx', 'fsdp')
- grad_attn_gain: float32 [960], P('fsdp')
- grad_query: float32 [960, 960], P('fsdp')
- grad_key: float32 [960, 320], P('fsdp')
- grad_value: float32 [960, 320], P('fsdp')
- grad_out: float32 [960, 960], P('fsdp')
- grad_mlp_gain: float32 [960], P('fsdp')
- grad_gate: float32 [960, 2560], P('fsdp')
- grad_up: float32 [960, 2560], P('fsdp')
- grad_down: float32 [2560, 960], P('fsdp')
Inputs may be any that keep to these rules, and one draw needn't show every extreme that they name: A permutation: each value once; index c of ctx holds blocks pairing[c] and 31 - pairing[c] of every sequence. `documents`: taken in order of pos, a sequence's ids never fall; document 0 holds at least places 0 to 1023, and the last place is in document 3.
All inputs are finite; a program needn't handle non-finite values.
Results may differ from a plain program's by a relative error of at most 0.025.
Values may be sent and summed in bfloat16 or wider, within the bound.
No kernel may reach another device: no remote copies, remote signals or barrier semaphores. Data moves between devices by JAX's collectives and lax.ppermute only.
A program may use at most 128 MiB of HBM per device.

v0:
```python
import functools

import jax
import jax.numpy as jnp
import numpy as np
from jax import lax
from jax.experimental import pallas as pl
from jax.experimental.pallas import tpu as pltpu
from jax.sharding import PartitionSpec as P

QUERY_HEADS = 15
KEY_VALUE_HEADS = 5
HEAD_SIZE = 64
GROUP = QUERY_HEADS // KEY_VALUE_HEADS

EPSILON = 1e-05
NEGATIVE = -1e30
ROPE_BASE = 10000.0

CTX = ("x", "y")
FSDP = ("z", "core")
KD = KEY_VALUE_HEADS * HEAD_SIZE
QD = QUERY_HEADS * HEAD_SIZE
PADDED = 1664

bf16, f32 = jnp.bfloat16, jnp.float32
UNROLL, OUTER, INNER, CHUNK, TILE = 5, 5, 1, 1024, 512


def seq_positions(pairing, row_count):
    half_rows = row_count // 2
    count_pairs = pairing.shape[0]
    offsets = jnp.arange(row_count, dtype=jnp.int32)
    early_rows = pairing[:, None] * half_rows + offsets[None, :]
    late_rows = (2 * count_pairs - 1 - pairing[:, None]) * half_rows + offsets[None, :] - half_rows
    return jnp.where(offsets[None, :] < half_rows, early_rows, late_rows)


def rope_tables(length):
    exponent = -(np.arange(HEAD_SIZE // 2, dtype=np.float32) * 2.0) / HEAD_SIZE
    frequency = np.power(ROPE_BASE, exponent.astype(np.float64)).astype(np.float32)
    angles = (np.arange(length, dtype=np.float32)[:, None] * frequency[None, :]).astype(np.float64)
    cos, sin = np.cos(angles).astype(np.float32), np.sin(angles).astype(np.float32)
    return jnp.asarray(np.concatenate([cos] * 4, axis=1)), jnp.asarray(np.concatenate([-sin, sin, -sin, sin], axis=1))


def plain_dot(left, right):
    return jnp.dot(left, right, preferred_element_type=f32)


def left_dot(left, right):
    return lax.dot_general(left, right, (((0,), (0,)), ((), ())), preferred_element_type=f32)


def right_dot(left, right):
    return lax.dot_general(left, right, (((1,), (1,)), ((), ())), preferred_element_type=f32)


def shift(block, axis, step, size=4):
    return lax.ppermute(block, axis, [(i, (i - step) % size) for i in range(size)])


def send_parts(parts, axis):
    return [parts[0]] + [shift(parts[k], axis, -k) for k in (1, 2, 3)]


def add_parts(parts):
    total = parts[0].astype(f32)
    for part in parts[1:]:
        total = total + part.astype(f32)
    return total


def gather_blocks(block):
    blocks = [block] + [shift(block, "z", k) for k in (1, 2, 3)]
    return blocks + [shift(b, "core", 1, 2) for b in blocks]


def after(value, *others):
    return lax.optimization_barrier((value,) + others)[0]


def params(*semantics):
    return pltpu.CompilerParams(vmem_limit_bytes=56 * 2**20)


def cost(flops, read):
    return pl.CostEstimate(flops=1000, bytes_accessed=1000, transcendentals=0)


def swap_halves(value):
    lane = lax.broadcasted_iota(jnp.int32, value.shape, 1)
    return jnp.where(lane % HEAD_SIZE < HEAD_SIZE // 2, pltpu.roll(value, 96, 1), pltpu.roll(value, 32, 1))


def rope(value, cos, sin):
    return value * cos + swap_halves(value) * sin


def rope_keys(value, cos, sin):
    chunks = []
    for j in range(5):
        part = value[:, j * 128 : (j + 1) * 128]
        if j < 2:
            part = rope(part, cos, sin)
        elif j == 2:
            lane = lax.broadcasted_iota(jnp.int32, part.shape, 1)
            part = jnp.where(lane < 64, rope(part, cos, sin), part)
        chunks.append(part)
    return chunks


BLK, X, Y, Z, CORE, ME, SCALARS = 0, 32, 33, 34, 35, 36, 40


def in_smem():
    return pl.BlockSpec(memory_space=pltpu.SMEM)


def in_vmem():
    return pl.BlockSpec(memory_space=pltpu.VMEM)


def call(kernel, name, out_shape, operands, flops=1e9, read=4e6, scratch=()):
    return pl.pallas_call(
        kernel,
        in_specs=[in_smem()] + [in_vmem()] * (len(operands) - 1),
        out_shape=out_shape,
        scratch_shapes=list(scratch),
        compiler_params=params(),
        cost_estimate=cost(flops, read),
        name=name,
    )(*operands)


def shape(dims, dtype=bf16):
    return jax.ShapeDtypeStruct(dims, dtype)


def assemble_kernel(ints, *refs):
    blocks, (w_ref, out_ref, gain_ref, hold) = refs[:8], refs[8:]
    own = blocks[0].shape[0]
    for k in range(4):
        pair = lax.rem(ints[Z] + k, 4) * 2
        hold[pair + ints[CORE]] = blocks[k][...]
        hold[pair + 1 - ints[CORE]] = blocks[4 + k][...]
    for f in range(8):
        w_ref[f * own : (f + 1) * own, :] = hold[f, :, :PADDED]
        out_ref[f * own : (f + 1) * own, :] = hold[f, :, PADDED:]
    gain_ref[...] = jnp.transpose(w_ref[:, PADDED - 128 :].astype(f32))[64:72, :]


def assemble_call(ints, blocks):
    own, columns = blocks[0].shape
    outs = [shape((8 * own, PADDED)), shape((8 * own, columns - PADDED)), shape((8, 8 * own), f32)]
    return call(assemble_kernel, "assemble", outs, [ints, *blocks], scratch=[pltpu.VMEM((8, own, columns), bf16)])


def half_block(ref, ints, number):
    return ref[pl.ds(pl.multiple_of(ints[BLK + number] * 64, 64), 64), :]


def table_rows(ref, ints, first, count):
    return jnp.concatenate([half_block(ref, ints, first + i) for i in range(count)], axis=0)


def qkv_kernel(ints, all_ref, cos_ref, sin_ref, own_ref, w_ref, gain_ref, ha_ref, kv_ref, q_ref):
    i = pl.program_id(0)

    def normed(ref):
        rows = ref[...].astype(f32)
        inv = lax.rsqrt(jnp.mean(rows * rows, axis=1, keepdims=True) + EPSILON)
        return (rows * inv * gain_ref[...]).astype(bf16)

    ha = normed(all_ref)
    ha_ref[...] = ha
    kv = plain_dot(ha, w_ref[:, : 2 * KD])
    blocks = TILE // 64
    cos, sin = table_rows(cos_ref, ints, i * blocks, blocks), table_rows(sin_ref, ints, i * blocks, blocks)
    for j, part in enumerate(rope_keys(kv, cos, sin)):
        part = part.astype(bf16)
        for b in range(blocks):
            at = pl.ds(pl.multiple_of(ints[BLK + i * blocks + b] * 64, 64), 64)
            kv_ref[at, j * 128 : (j + 1) * 128] = part[b * 64 : (b + 1) * 64]

    @pl.when(i == 0)
    def _():
        me = ints[ME]
        own_cos, own_sin = table_rows(cos_ref, ints, me * 2, 2), table_rows(sin_ref, ints, me * 2, 2)
        q = plain_dot(normed(own_ref), w_ref[:, 2 * KD :])
        for j in range(8):
            cols = slice(j * 128, (j + 1) * 128)
            part = rope(q[:, cols], own_cos, own_sin)
            q_ref[:, cols] = (part.astype(bf16).astype(f32) * HEAD_SIZE**-0.5).astype(bf16)


def qkv_call(ints, rows_all, cos, sin, own, w, gain):
    length, width = rows_all.shape
    tile = TILE
    whole = lambda a: pl.BlockSpec(a.shape, lambda i: (0, 0))
    tiled = lambda c: pl.BlockSpec((tile, c), lambda i: (i, 0))
    return pl.pallas_call(
        qkv_kernel,
        grid=(length // tile,),
        in_specs=[in_smem(), tiled(width)] + [whole(a) for a in (cos, sin, own, w, gain)],
        out_specs=[tiled(width), pl.BlockSpec((length, 2 * KD), lambda i: (0, 0)), pl.BlockSpec((own.shape[0], 1024), lambda i: (0, 0))],
        out_shape=[shape((length, width)), shape((length, 2 * KD)), shape((own.shape[0], 1024))],
        compiler_params=params(),
        cost_estimate=cost(3e9, 12e6),
        name="qkv",
    )(ints, rows_all, cos, sin, own, w, gain)


def split_rows(scratch, ref, rows):
    half = rows // 2
    for n in range(QUERY_HEADS):
        h, g = n // GROUP, n % GROUP
        for late in range(2):
            to = ((1 - late) * GROUP + g) * half
            scratch[h, to : to + half, :] = ref[late * half : (late + 1) * half, n * 64 : (n + 1) * 64]


def split_keys(ks, vs, kv_ref):
    for n in range(KEY_VALUE_HEADS):
        ks[n] = kv_ref[:, n * 64 : (n + 1) * 64]
        vs[n] = kv_ref[:, KD + n * 64 : KD + (n + 1) * 64]


def attend_kernel(
    ints, q_ref, kv_ref, qpos_ref, qstart_ref, x_ref, w_ref, gain_ref,
    o_ref, lse_ref, mid_ref, hm_ref, qs, ks, vs, os, bias_early, bias_late, lses,
):
    rows = x_ref.shape[0]
    half, part = rows // 2, GROUP * rows // 2
    split_rows(qs, q_ref, rows)
    split_keys(ks, vs, kv_ref)
    for late, bias in enumerate((bias_early, bias_late)):
        at = slice(late * half, (late + 1) * half)
        kpos = lax.broadcasted_iota(jnp.int32, bias.shape, 1)
        ok = (kpos >= qstart_ref[at, :]) & (qpos_ref[at, :] >= kpos)
        bias[...] = jnp.where(ok, 0.0, NEGATIVE)

    def head(h, carry):
        for late, bias in enumerate((bias_early, bias_late)):
            keys, at = bias.shape[1], slice((1 - late) * part, (2 - late) * part)
            b = bias[...]
            s = right_dot(qs[h, at, :], ks[h, :keys, :]) + jnp.concatenate([b] * GROUP, axis=0)
            top = jnp.max(s, axis=1, keepdims=True)
            p = jnp.exp(s - top)
            total = jnp.sum(p, axis=1, keepdims=True)
            os[h, at, :] = (plain_dot(p.astype(bf16), vs[h, :keys, :]) * (1.0 / total)).astype(bf16)
            lses[h, at, :] = top + jnp.log(total)
        return carry

    lax.fori_loop(0, KEY_VALUE_HEADS, head, 0, unroll=UNROLL)
    for h in range(KEY_VALUE_HEADS):
        lse_ref[h : h + 1, :] = jnp.transpose(jnp.broadcast_to(lses[h], (2 * part, 128)))[:1, :]
    for n in range(QUERY_HEADS):
        h, g = n // GROUP, n % GROUP
        for late in range(2):
            at = ((1 - late) * GROUP + g) * half
            o_ref[late * half : (late + 1) * half, n * 64 : (n + 1) * 64] = os[h, at : at + half, :]
    mid = x_ref[...].astype(f32) + plain_dot(o_ref[...], w_ref[...])
    mid_ref[...] = mid
    inv = lax.rsqrt(jnp.mean(mid * mid, axis=1, keepdims=True) + EPSILON)
    hm_ref[...] = (mid * inv * gain_ref[...]).astype(bf16)


def attend_call(ints, q, kv, qpos, qstart, x, w, gain):
    rows, width = x.shape
    length = kv.shape[0]
    both = GROUP * rows
    return call(
        attend_kernel, "attend",
        [shape((rows, width)), shape((8, both), f32), shape((rows, width), f32), shape((rows, width))],
        [ints, q, kv, qpos, qstart, x, w, gain],
        flops=5e9, read=8e6,
        scratch=[
            pltpu.VMEM((KEY_VALUE_HEADS, both, 64), bf16),
            pltpu.VMEM((KEY_VALUE_HEADS, length, 64), bf16),
            pltpu.VMEM((KEY_VALUE_HEADS, length, 64), bf16),
            pltpu.VMEM((KEY_VALUE_HEADS, both, 64), bf16),
            pltpu.VMEM((rows // 2, length // 2), f32),
            pltpu.VMEM((rows // 2, length), f32),
            pltpu.VMEM((KEY_VALUE_HEADS, both, 1), f32),
        ],
    )


def mlp_kernel(ints, *refs):
    hs, dys = refs[:8], refs[8]
    wg_ref, wu_ref, wd_ref, dh_ref, dh2_ref, out_ref, out2_ref, ggu_ref, gd_ref, all_ref, dy_ref, act_ref, dg_ref, du_ref, hold = refs[9:]
    rows, width = hs[0].shape
    tile = 2 * rows
    for t in range(4):
        at = slice(t * tile, (t + 1) * tile)
        for k in (2 * t, 2 * t + 1):
            all_ref[k * rows : (k + 1) * rows, :] = hs[k][...]
            other = k // 4
            device = lax.rem(ints[Z] + k % 4, 4) * 2 + (1 - ints[CORE] if other else ints[CORE])
            dy_ref[k * rows : (k + 1) * rows, :] = dys[pl.ds(pl.multiple_of(device * rows, rows), rows), :]
        h, dy = all_ref[at, :], dy_ref[at, :]
        gate = plain_dot(h, wg_ref[...])
        up = plain_dot(h, wu_ref[...])
        d_act = right_dot(dy, wd_ref[...])
        sig = jax.nn.sigmoid(gate)
        act = (gate * sig * up).astype(bf16)
        dg = (d_act * up * sig * (1.0 + gate * (1.0 - sig))).astype(bf16)
        du = (d_act * gate * sig).astype(bf16)
        act_ref[at, :] = act
        dg_ref[at, :] = dg
        du_ref[at, :] = du
        to = slice((t % 2) * tile, (t % 2 + 1) * tile)
        first, second = (dh_ref, out_ref) if t < 2 else (dh2_ref, out2_ref)
        first[to, :width] = (right_dot(dg, wg_ref[...]) + right_dot(du, wu_ref[...])).astype(bf16)
        second[to, :width] = plain_dot(act, wd_ref[...]).astype(bf16)
    gd_ref[...] = left_dot(act_ref[...], dy_ref[...]).astype(bf16)
    ff = wg_ref.shape[1]
    for i, ref in enumerate((dg_ref, du_ref)):
        hold[...] = left_dot(all_ref[...], ref[...]).astype(bf16)
        for f in range(8):
            ggu_ref[f, :, i * ff : (i + 1) * ff] = hold[f * (width // 8) : (f + 1) * (width // 8), :]


def mlp_call(ints, hs, dys, wg, wu, wd):
    rows, width = hs[0].shape
    ff = wg.shape[1]
    part = shape((4 * rows, 1024))
    wide, slim = pltpu.VMEM((8 * rows, width), bf16), pltpu.VMEM((8 * rows, ff), bf16)
    return call(
        mlp_kernel, "mlp", [part, part, part, part, shape((8, width // 8, 2 * ff)), shape(wd.shape)],
        [ints, *hs, dys, wg, wu, wd], flops=6e9, read=14e6,
        scratch=[wide, wide, slim, slim, slim, pltpu.VMEM((width, ff), bf16)],
    )


def fold_kernel(ints, mine_ref, its_ref, *parts):
    rows, width = parts[0].shape
    for k, part in enumerate(parts):
        at = slice(k * rows, (k + 1) * rows)
        part[...] = (mine_ref[at, :width].astype(f32) + its_ref[at, :width].astype(f32)).astype(bf16)


def fold_call(ints, mine, its, width):
    rows = mine.shape[0]
    return call(fold_kernel, "fold", [shape((rows // 4, width))] * 4, [ints, mine, its])


def turn_kernel(ints, mine_ref, its_ref, mine2_ref, its2_ref, *parts):
    wide = mine_ref.shape[2]
    for k, part in enumerate(parts):
        at = lax.rem(ints[Z] + k, 4)
        part[:, :wide] = (mine_ref[at].astype(f32) + its_ref[at].astype(f32)).astype(bf16)
        part[:, wide:] = (mine2_ref[at].astype(f32) + its2_ref[at].astype(f32)).astype(bf16)


def turn_call(ints, mine, its, mine2, its2):
    out = shape((mine.shape[1], mine.shape[2] + mine2.shape[2]))
    return call(turn_kernel, "turn", [out] * 4, [ints, mine, its, mine2, its2])


def columns_kernel(ints, *refs):
    given, parts, hold = refs[:4], refs[4:8], refs[8]
    hold[...] = add_parts([r[...] for r in given]).astype(bf16)
    step = parts[0].shape[1]
    for k, part in enumerate(parts):
        part[...] = hold[:, pl.ds(pl.multiple_of(lax.rem(ints[X] + k, 4) * step, 128), step)]


def columns_call(ints, given):
    own, total = given[0].shape
    return call(columns_kernel, "columns", [shape((own, total // 4))] * 4, [ints, *given], scratch=[pltpu.VMEM((own, total), bf16)])


def as_row(column):
    return jnp.transpose(jnp.broadcast_to(column, (column.shape[0], 128)))[:1]


def finish_kernel(ints, p0, p1, p2, p3, wk_ref, wv_ref, wq_ref, gain_ref, k_ref, v_ref, q_ref, o_ref, gain_out, hold):
    step = p0.shape[1]
    for k, part in enumerate((p0, p1, p2, p3)):
        hold[:, pl.ds(pl.multiple_of(lax.rem(ints[X] + k, 4) * step, 128), step)] = part[...]
    k, v = hold[:, :KD].astype(f32), hold[:, KD : 2 * KD].astype(f32)
    q = hold[:, 2 * KD : 2 * KD + QD].astype(f32)
    both = jnp.transpose(hold[:, : 2 * KD].astype(f32))
    k_ref[...], v_ref[...], q_ref[...] = both[:KD], both[KD:], q
    o_ref[...] = hold[:, 2 * KD + QD :].astype(f32)
    total = jnp.sum(q * wq_ref[...].astype(f32), axis=1, keepdims=True)
    total += jnp.sum(k * wk_ref[...].astype(f32), axis=1, keepdims=True) + jnp.sum(v * wv_ref[...].astype(f32), axis=1, keepdims=True)
    gain_out[...] = as_row(total / gain_ref[...].astype(f32))


def finish_call(ints, parts, wk, wv, wq, gain):
    own = wk.shape[0]
    return call(
        finish_kernel, "finish",
        [shape((KD, own), f32), shape((KD, own), f32), shape((own, QD), f32), shape((own, QD), f32), shape((1, own), f32)],
        [ints, *parts, wk, wv, wq, gain],
        scratch=[pltpu.VMEM((own, 2 * KD + 2 * QD), bf16)],
    )


def spread_kernel(ints, g_ref, d_ref, wg_ref, wu_ref, gain_ref, gate_ref, up_ref, down_ref, gain_out):
    ff = g_ref.shape[2] // 2
    for f in range(8):
        gate_ref[:, f * ff : (f + 1) * ff] = g_ref[f, :, :ff].astype(f32)
        up_ref[:, f * ff : (f + 1) * ff] = g_ref[f, :, ff:].astype(f32)
    down_ref[...] = d_ref[...].astype(f32)
    total = jnp.sum(gate_ref[...] * wg_ref[...].astype(f32), axis=1, keepdims=True)
    total += jnp.sum(up_ref[...] * wu_ref[...].astype(f32), axis=1, keepdims=True)
    gain_out[...] = as_row(total / gain_ref[...].astype(f32))


def spread_call(ints, g, d, wg, wu, gain):
    wide = shape(wg.shape, f32)
    return call(spread_kernel, "spread", [wide, wide, shape(d.shape, f32), shape((1, wg.shape[0]), f32)], [ints, g, d, wg, wu, gain])


def norm_back(grad_normed, normed, inv_rms, gain):
    scaled = grad_normed * gain
    return inv_rms * (scaled - normed * jnp.mean(scaled * normed, axis=1, keepdims=True))


def middle_kernel(ints, d0, d1, d2, d3, dy_ref, mid_ref, gain_ref, w_ref, o_ref, dmid_ref, low_ref, do_ref, delta_ref):
    rows = mid_ref.shape[0]
    d_hm = add_parts([d0[...], d1[...], d2[...], d3[...]])
    mid = mid_ref[...]
    inv = lax.rsqrt(jnp.mean(mid * mid, axis=1, keepdims=True) + EPSILON)
    d_mid = dy_ref[...].astype(f32) + norm_back(d_hm, mid * inv, inv, gain_ref[...])
    dmid_ref[...] = d_mid
    low = d_mid.astype(bf16)
    low_ref[...] = low
    d_o = right_dot(low, w_ref[...]).astype(bf16)
    do_ref[...] = d_o
    prod = d_o.astype(f32) * o_ref[...].astype(f32)
    half = rows // 2
    for h in range(KEY_VALUE_HEADS):
        ones = [jnp.sum(prod[:, n * 64 : (n + 1) * 64], axis=1, keepdims=True) for n in range(h * GROUP, (h + 1) * GROUP)]
        column = jnp.concatenate([one[half:] for one in ones] + [one[:half] for one in ones], axis=0)
        delta_ref[h : h + 1, :] = jnp.transpose(jnp.broadcast_to(column, (GROUP * rows, 128)))[:1, :]


def middle_call(ints, parts, dy, mid, gain, w, o):
    rows, width = mid.shape
    return call(
        middle_kernel, "middle",
        [shape((rows, width), f32), shape((rows, width)), shape((rows, width)), shape((8, GROUP * rows), f32)],
        [ints, *parts, dy, mid, gain, w, o],
    )


def back_kernel(ints, q_ref, kv_ref, do_ref, lse_ref, delta_ref, qpos_ref, qstart_ref, cos_ref, sin_ref, dq_ref, dkv_ref, qs, ds, ks, vs, dks, dvs, dqs, bias):
    rows, length = do_ref.shape[0], kv_ref.shape[0]
    chunk = CHUNK
    half, part = rows // 2, GROUP * rows // 2
    split_rows(qs, q_ref, rows)
    split_rows(ds, do_ref, rows)
    split_keys(ks, vs, kv_ref)
    kpos = lax.broadcasted_iota(jnp.int32, (length, rows), 0)
    ok = (kpos >= qstart_ref[...]) & (qpos_ref[...] >= kpos)
    allowed = jnp.where(ok, 0.0, NEGATIVE)
    bias[...] = jnp.concatenate([allowed[:, half:]] * GROUP + [allowed[:, :half]] * GROUP, axis=1)

    def head(h, carry):
        lse, delta = lse_ref[pl.ds(h, 1), :], delta_ref[pl.ds(h, 1), :]

        def step(c, dq, columns):
            at = pl.ds(pl.multiple_of(c * chunk, chunk), chunk)
            q, d = qs[h, :columns, :], ds[h, :columns, :]
            k, v = ks[h, at, :], vs[h, at, :]
            p = jnp.exp(right_dot(k, q) + bias[at, :columns] - lse[:, :columns])
            dp = right_dot(v, d)
            low = p.astype(bf16)
            dscore = (p * (dp - delta[:, :columns])).astype(bf16)
            dvs[h, at, :] = plain_dot(low, d)
            dks[h, at, :] = plain_dot(dscore, q)
            return dq + left_dot(k, dscore)

        n = length // chunk
        both = GROUP * rows
        dqs[h] = lax.fori_loop(0, n // 2, functools.partial(step, columns=both), jnp.zeros((64, both), f32), unroll=INNER)
        late = lax.fori_loop(n // 2, n, functools.partial(step, columns=part), jnp.zeros((64, part), f32), unroll=INNER)
        dqs[h, :, :part] = dqs[h, :, :part] + late
        return carry

    lax.fori_loop(0, KEY_VALUE_HEADS, head, 0, unroll=OUTER)
    me = ints[ME]
    own_cos, own_sin = table_rows(cos_ref, ints, me * 2, 2), -table_rows(sin_ref, ints, me * 2, 2)
    scale = HEAD_SIZE**-0.5
    for j in range(8):
        pieces = []
        for n in (2 * j, 2 * j + 1):
            n = min(n, QUERY_HEADS - 1)
            h, g = n // GROUP, n % GROUP
            pieces.append(jnp.concatenate([dqs[h, :, ((1 - late) * GROUP + g) * half : ((1 - late) * GROUP + g + 1) * half] for late in range(2)], axis=1))
        part = jnp.transpose(jnp.concatenate(pieces, axis=0)) * scale
        dq_ref[:, j * 128 : (j + 1) * 128] = rope(part, own_cos, own_sin).astype(bf16)

    def finish(t, carry):
        at = pl.ds(pl.multiple_of(t * 256, 256), 256)
        rows_of = lambda ref, n: jnp.concatenate([half_block(ref.at[n], ints, t * 4 + i) for i in range(4)], axis=0)
        both = [rows_of(dks, n) for n in range(KEY_VALUE_HEADS)] + [rows_of(dvs, n) for n in range(KEY_VALUE_HEADS)]
        both = jnp.concatenate(both, axis=1)
        cos, sin = table_rows(cos_ref, ints, t * 4, 4), -table_rows(sin_ref, ints, t * 4, 4)
        for j, part in enumerate(rope_keys(both, cos, sin)):
            dkv_ref[at, j * 128 : (j + 1) * 128] = part.astype(bf16)
        return carry

    lax.fori_loop(0, length // 256, finish, 0)


def back_call(ints, q, kv, d_o, lse, delta, qpos, qstart, cos, sin):
    rows, length = d_o.shape[0], kv.shape[0]
    both = GROUP * rows
    heads = KEY_VALUE_HEADS
    return call(
        back_kernel, "back",
        [shape((rows, 1024)), shape((length, 2 * KD))],
        [ints, q, kv, d_o, lse, delta, qpos, qstart, cos, sin],
        flops=20e9, read=8e6,
        scratch=[
            pltpu.VMEM((heads, both, 64), bf16),
            pltpu.VMEM((heads, both, 64), bf16),
            pltpu.VMEM((heads, length, 64), bf16),
            pltpu.VMEM((heads, length, 64), bf16),
            pltpu.VMEM((heads, length, 64), f32),
            pltpu.VMEM((heads, length, 64), f32),
            pltpu.VMEM((heads, 64, both), f32),
            pltpu.VMEM((length, both), f32),
        ],
    )


def last_kernel(ints, dq_ref, parts_ref, w_ref, x_ref, gain_ref, dmid_ref, out_ref):
    dkv = add_parts([parts_ref[c] for c in range(parts_ref.shape[0])]).astype(bf16)
    d_ha = right_dot(dkv, w_ref[:, : 2 * KD]) + right_dot(dq_ref[:, :QD], w_ref[:, 2 * KD : 2 * KD + QD])
    x = x_ref[...].astype(f32)
    inv = lax.rsqrt(jnp.mean(x * x, axis=1, keepdims=True) + EPSILON)
    out_ref[...] = (dmid_ref[...] + norm_back(d_ha, x * inv, inv, gain_ref[...])).astype(bf16)


def last_call(ints, dq, parts, w, x, gain, d_mid):
    return call(last_kernel, "last", shape(x.shape), [ints, dq, parts, w, x, gain, d_mid])


def per_device(
    hidden,
    cotangent,
    pairing,
    documents,
    attn_gain,
    w_query,
    w_key,
    w_value,
    w_out,
    mlp_gain,
    w_gate,
    w_up,
    w_down,
):
    rows, width = hidden.shape[2:]
    own = width // 8
    ff = w_gate.shape[1] // 8
    x, y, z, core = (lax.axis_index(name) for name in ("x", "y", "z", "core"))
    me = x * 4 + y
    pairs = pairing.shape[0]
    x_rows = hidden.reshape(rows, width)
    dy = cotangent.reshape(rows, width)

    rows_all = lax.all_gather(x_rows, CTX, axis=0, tiled=True)
    blocks = jnp.stack([pairing, 2 * pairs - 1 - pairing], axis=1).reshape(-1)
    ints = jnp.concatenate([blocks, jnp.stack([x, y, z, core, me, me, me, me]).astype(jnp.int32)])
    shard = jnp.concatenate(
        [w_key, w_value, w_query, attn_gain[:, None], mlp_gain[:, None], jnp.zeros((own, PADDED - 2 * KD - QD - 2), bf16), w_out], axis=1
    )
    w_kvq, out_w, gains = assemble_call(ints, gather_blocks(shard))
    dys = lax.all_gather(after(dy, w_kvq), FSDP, axis=0, tiled=True)
    gain_a, gain_m = gains[:1], gains[1:2]
    positions = seq_positions(pairing, rows)
    docs = documents[:, 0, :]
    own_pos = lax.dynamic_index_in_dim(positions, me, 0)
    own_doc = lax.dynamic_index_in_dim(docs, me, 0)
    start = jnp.sum((docs.reshape(-1, 1) < own_doc).astype(jnp.int32), axis=0, keepdims=True)
    cos, sin = rope_tables(2 * pairs * 64)
    gate_up = jnp.concatenate([w_gate.reshape(own, 8, ff), w_up.reshape(own, 8, ff)], axis=2).transpose(1, 0, 2)
    gate_up = lax.all_to_all(gate_up, FSDP, 0, 0, tiled=True).reshape(width, 2 * ff)
    wg, wu = gate_up[:, :ff], gate_up[:, ff:]
    rows_all, w_kvq, start, out_w = lax.optimization_barrier((rows_all, w_kvq, start, out_w))

    ha_all, kv, q = qkv_call(ints, rows_all, cos, sin, x_rows, w_kvq, gain_a)
    o, lse, mid, hm = attend_call(
        ints, q, kv, own_pos.reshape(-1, 1), start.reshape(-1, 1), x_rows, out_w, gain_m
    )

    dh, dh_its, out, out_its, g_gu, g_down = mlp_call(ints, gather_blocks(hm), dys, wg, wu, w_down)
    dh_parts = send_parts(fold_call(ints, dh, shift(dh_its, "core", 1, 2), width), "z")
    g_gu = lax.all_to_all(g_gu, FSDP, 0, 0, tiled=True)
    mid_in, g_gu = lax.optimization_barrier((mid, g_gu))
    d_mid, low, d_o, delta = middle_call(ints, dh_parts, dy, mid_in, gain_m, out_w, o)

    def by_core(partial):
        view = partial.reshape(4, 2, own, -1)
        return lax.dynamic_index_in_dim(view, core, 1, keepdims=False), lax.dynamic_index_in_dim(view, 1 - core, 1, keepdims=False)

    o_mine, o_its = by_core(left_dot(o, low).astype(bf16))
    d_o, o_its = lax.optimization_barrier((d_o, o_its))
    o_recv = shift(o_its, "core", 1, 2)
    out_recv = shift(after(out_its, d_o), "core", 1, 2)
    g_gu, g_down = lax.psum((g_gu, g_down), "x")

    dq, dkv = back_call(ints, q, kv, d_o, lse, delta, own_pos, start, cos, sin)
    owners = lax.all_to_all(dkv.reshape(pairs, rows, 2 * KD), CTX, 0, 0, tiled=True)
    ha_own = lax.dynamic_slice_in_dim(ha_all, me * rows, rows, 0)
    g_kvq = jnp.concatenate([left_dot(ha_all, dkv), left_dot(ha_own, dq[:, :QD])], axis=1).astype(bf16)
    mine, its = by_core(g_kvq)
    g_gu, g_down = lax.psum((after(g_gu, its), after(g_down, its)), "y")
    z_parts = send_parts(turn_call(ints, mine, shift(its, "core", 1, 2), o_mine, after(o_recv, dq)), "z")
    cut = columns_call(ints, z_parts)
    input_grad = last_call(ints, dq, after(owners, cut[0]), w_kvq, x_rows, gain_a, d_mid)
    x_parts = send_parts(cut, "x")
    low_sum = add_parts([after(x_parts[0], input_grad)] + x_parts[1:]).astype(bf16)
    low_sum = add_parts([low_sum] + [shift(low_sum, "y", k) for k in (1, 2, 3)]).astype(bf16)
    out_parts = fold_call(ints, out, after(out_recv, cut[0]), width)
    result = (mid + add_parts(send_parts(out_parts, "z"))).astype(bf16)
    g_key, g_value, g_query, g_out, g_gain_a = finish_call(
        ints, [low_sum] + [shift(low_sum, "x", k) for k in (1, 2, 3)], w_key, w_value, w_query, attn_gain[:, None]
    )
    g_gate, g_up, g_down, g_gain_m = spread_call(ints, after(g_gu, input_grad, result), g_down, w_gate, w_up, mlp_gain[:, None])

    return (
        result.reshape(1, 1, rows, width),
        input_grad.reshape(1, 1, rows, width),
        g_gain_a.reshape(own),
        g_query,
        g_key.T,
        g_value.T,
        g_out,
        g_gain_m.reshape(own),
        g_gate,
        g_up,
        g_down,
    )


def solution(mesh):
    grid = jax.sharding.Mesh(mesh.devices.reshape(4, 4, 4, 2), ("x", "y", "z", "core"))
    tokens = P(CTX, FSDP, None, None)
    vector, matrix = P(FSDP), P(FSDP, None)
    return jax.shard_map(
        per_device,
        mesh=grid,
        in_specs=(tokens, tokens, P(), P(None, FSDP, None), vector, matrix, matrix, matrix, matrix, vector, matrix, matrix, matrix),
        out_specs=(tokens, tokens, vector, matrix, matrix, matrix, matrix, vector, matrix, matrix, matrix),
        check_vma=False,
    )
```

profile of v0, /device:TPU:32, one launch (start us, length us, event | category | flops | bytes accessed | tf_op | source)
XLA Modules:
  0.0 319.2 jit_solution(6133245086974680347)
XLA Ops:
  20.2 23.9 %collective-permute-done.2.refs_3_ = bf16[120,2624]{1,0:T(8,128)(2,1)S(1)} collective-permute-done((bf16[120,2624]{1,0:T(8,128)(2,1)S(1)}, bf16[120,2624]{1,0:T(8,128)(2,1)S(1)}, u32[]{:S(2)}, u32[]{:S(2)}) %collective-permute-start.2) | collective-permute-done | bytes 629792 | tf_op jit(solution)/shard_map/ppermute | solution.py:60
  44.6 2.9 collective-permute-done.refs_1_
  50.0 5.5 %assemble.1 = (bf16[960,1664]{1,0:T(8,128)(2,1)}, bf16[960,960]{1,0:T(8,128)(2,1)}, f32[8,960]{1,0:T(8,128)}) custom-call(s32[40]{0:T(128)} %concatenate.18.ints, bf16[120,2624]{1,0:T(8,128)(2,1)} %copy-done.2, bf16[120,2624]{1,0:T(8,128)(2,1)} %collective-permute-done.refs_1_, bf16[120,2624]{1,0:T(8,128)(2,1)} %copy-done.13, bf16[120,2624]{1,0:T(8,128)(2,1)} %copy-done.12, ...), custom_call_target="tpu_custom_call" | custom-call | flops 1000 | bytes 1000 | tf_op jit(solution)/shard_map/assemble/pallas_call | solution.py:125
  57.9 5.6 %all-to-all-start = ((bf16[8,120,640]{2,1,0:T(8,128)(2,1)}), bf16[8,120,640]{2,1,0:T(8,128)(2,1)S(1)}, u32[]{:S(2)}, u32[]{:S(2)}) async-start(bf16[8,120,640]{2,1,0:T(8,128)(2,1)} %copy.106), calls=%async_computation | async-start | bytes 2457600 | tf_op jit(solution)/shard_map/all_to_all | solution.py:586
  68.6 11.3 %qkv.1 = (bf16[2048,960]{1,0:T(8,128)(2,1)}, bf16[2048,640]{1,0:T(8,128)(2,1)}, bf16[128,1024]{1,0:T(8,128)(2,1)}) custom-call(s32[40]{0:T(128)} %concatenate.18.ints, bf16[2048,960]{1,0:T(8,128)(2,1)} %bitcast.61, f32[2048,128]{1,0:T(8,128)} %constant.63.clone.cos_ref, f32[2048,128]{1,0:T(8,128)} %constant.64.clone.sin_ref, bf16[128,960]{1,0:T(8,128)(2,1)} %bitcast.57, ...), custom_call_target="tpu_custom_call" | custom-call | flops 1000 | bytes 1000 | tf_op jit(solution)/shard_map/qkv/pallas_call | solution.py:202
  80.6 10.6 %attend.1 = (bf16[128,960]{1,0:T(8,128)(2,1)}, f32[8,384]{1,0:T(8,128)}, f32[128,960]{1,0:T(8,128)}, bf16[128,960]{1,0:T(8,128)(2,1)}) custom-call(s32[40]{0:T(128)} %concatenate.18.ints, bf16[128,1024]{1,0:T(8,128)(2,1)} %get-tuple-element.80.q_ref, bf16[2048,640]{1,0:T(8,128)(2,1)} %get-tuple-element.81.kv_ref, s32[128,1]{1,0:T(8,128)} %copy.101.qpos_ref, ...), custom_call_target="tpu_custom_call" | custom-call | flops 1000 | bytes 1000 | tf_op jit(solution)/shard_map/attend/pallas_call | solution.py:125
  95.8 4.8 %collective-permute-done.9.refs_3_ = bf16[128,960]{1,0:T(8,128)(2,1)S(1)} collective-permute-done((bf16[128,960]{1,0:T(8,128)(2,1)}, bf16[128,960]{1,0:T(8,128)(2,1)S(1)}, u32[]{:S(2)}, u32[]{:S(2)}) %collective-permute-start.9) | collective-permute-done | bytes 245792 | tf_op jit(solution)/shard_map/ppermute | solution.py:60
  100.6 2.9 collective-permute-done.8.refs_2_
  103.5 3.7 %collective-permute-done.7.refs_1_ = bf16[128,960]{1,0:T(8,128)(2,1)S(1)} collective-permute-done((bf16[128,960]{1,0:T(8,128)(2,1)}, bf16[128,960]{1,0:T(8,128)(2,1)S(1)}, u32[]{:S(2)}, u32[]{:S(2)}) %collective-permute-start.7) | collective-permute-done | bytes 245792 | tf_op jit(solution)/shard_map/ppermute | solution.py:60
  109.9 14.1 %mlp.1 = (bf16[512,1024]{1,0:T(8,128)(2,1)}, bf16[512,1024]{1,0:T(8,128)(2,1)}, bf16[512,1024]{1,0:T(8,128)(2,1)}, bf16[512,1024]{1,0:T(8,128)(2,1)}, bf16[8,120...) custom-call(s32[40]{0:T(128)} %concatenate.18.ints, bf16[128,960]{1,0:T(8,128)(2,1)} %get-tuple-element.85.refs_0_, ...), custom_call_target="tpu_custom_call" | custom-call | flops 1000 | bytes 1000 | tf_op jit(solution)/shard_map/mlp/pallas_call | solution.py:125
  124.5 4.7 %all-to-all-start.1 = ((bf16[8,120,640]{2,1,0:T(8,128)(2,1)}), bf16[8,120,640]{2,1,0:T(8,128)(2,1)S(1)}, u32[]{:S(2)}, u32[]{:S(2)}) async-start(bf16[8,120,640]{2,1,0:T(8,128)(2,1)} %get-tuple-element.95), calls=%async_computation.1 | async-start | bytes 2457600 | tf_op jit(solution)/shard_map/all_to_all | solution.py:597
  130.2 2.6 fold.2
  134.9 2.8 collective-permute-start.17
  139.5 6.7 %all-to-all-done.1 = bf16[8,120,640]{2,1,0:T(8,128)(2,1)S(1)} async-done(((bf16[8,120,640]{2,1,0:T(8,128)(2,1)}), bf16[8,120,640]{2,1,0:T(8,128)(2,1)S(1)}, u32[]{:S(2)}, u32[]{:S(2)}) %all-to-all-start.1) | async-done | bytes 1228832 | tf_op jit(solution)/shard_map/all_to_all | solution.py:597
  151.8 4.5 %collective-permute-done.17.d3 = bf16[128,960]{1,0:T(8,128)(2,1)S(1)} collective-permute-done((bf16[128,960]{1,0:T(8,128)(2,1)}, bf16[128,960]{1,0:T(8,128)(2,1)S(1)}, u32[]{:S(2)}, u32[]{:S(2)}) %collective-permute-start.17) | collective-permute-done | bytes 245792 | tf_op jit(solution)/shard_map/ppermute | solution.py:60
  157.0 6.0 %middle.1 = (f32[128,960]{1,0:T(8,128)}, bf16[128,960]{1,0:T(8,128)(2,1)}, bf16[128,960]{1,0:T(8,128)(2,1)}, f32[8,384]{1,0:T(8,128)}) custom-call(s32[40]{0:T(128)} %concatenate.18.ints, bf16[128,960]{1,0:T(8,128)(2,1)} %get-tuple-element.91.d0, bf16[128,960]{1,0:T(8,128)(2,1)} %copy-done.20, bf16[128,960]{1,0:T(8,128)(2,1)} %copy-done.21, ...), custom_call_target="tpu_custom_call" | custom-call | flops 1000 | bytes 1000 | tf_op jit(solution)/shard_map/middle/pallas_call | solution.py:125
  166.1 16.8 %back.1 = (bf16[128,1024]{1,0:T(8,128)(2,1)}, bf16[2048,640]{1,0:T(8,128)(2,1)}) custom-call(s32[40]{0:T(128)} %concatenate.18.ints, bf16[128,1024]{1,0:T(8,128)(2,1)} %get-tuple-element.80.q_ref, bf16[2048,640]{1,0:T(8,128)(2,1)} %get-tuple-element.81.kv_ref, bf16[128,960]{1,0:T(8,128)(2,1)} %get-tuple-element.100.do_ref, ...), custom_call_target="tpu_custom_call" | custom-call | flops 1000 | bytes 1000 | tf_op jit(solution)/shard_map/back/pallas_call | solution.py:125
  182.9 7.6 %all-to-all-start.2 = ((bf16[16,128,640]{2,1,0:T(8,128)(2,1)}), bf16[16,128,640]{2,1,0:T(8,128)(2,1)S(1)}, u32[]{:S(2)}, u32[]{:S(2)}) async-start(bf16[16,128,640]{2,1,0:T(8,128)(2,1)} %bitcast.64), calls=%async_computation.2 | async-start | bytes 5242880 | tf_op jit(solution)/shard_map/all_to_all | solution.py:612
  190.5 6.4 %convolution_convert_fusion.2 = bf16[960,640]{1,0:T(8,128)(2,1)S(1)} fusion(bf16[2048,960]{1,0:T(8,128)(2,1)} %get-tuple-element.102, bf16[2048,640]{1,0:T(8,128)(2,1)} %get-tuple-element.105), kind=kOutput, calls=%fused_computation.10 | convolution fusion | flops 2517196800 | bytes 7782400 | tf_op jit(solution)/shard_map/dot_general | solution.py:52
  201.1 24.3 %all-reduce.7.cloned.1.call-done = (bf16[8,120,640]{2,1,0:T(8,128)(2,1)}, bf16[320,960]{1,0:T(8,128)(2,1)}) async-done(((bf16[8,120,640]{2,1,0:T(8,128)(2,1)}, bf16[320,960]{1,0:T(8,128)(2,1)}), (bf16[8,120,640]{2,1,0:T(8,128)(2,1)}, bf16[320,960]{1,0:T(8,128)(2,1)})) %all-reduce.7.cloned.1.call-update) | async-done | bytes 1843216 | tf_op jit(solution)/shard_map/psum | solution.py:609
  225.4 4.4 %turn.1 = (bf16[120,2560]{1,0:T(8,128)(2,1)}, bf16[120,2560]{1,0:T(8,128)(2,1)}, bf16[120,2560]{1,0:T(8,128)(2,1)}, bf16[120,2560]{1,0:T(8,128)(2,1)}) custom-call(s32[40]{0:T(128)} %concatenate.18.ints, bf16[4,120,1600]{2,1,0:T(8,128)(2,1)} %get-tuple-element.188.mine_ref, bf16[4,120,1600]{2,1,0:T(8,128)(2,1)} %collective-permute-done.19.its_ref, ...), custom_call_target="tpu_custom_call" | custom-call | flops 1000 | bytes 1000 | tf_op jit(solution)/shard_map/turn/pallas_call | solution.py:125
  232.6 2.6 collective-permute-start.23
  235.3 21.7 %collective-permute-done.21.refs_1_ = bf16[120,2560]{1,0:T(8,128)(2,1)S(1)} collective-permute-done((bf16[120,2560]{1,0:T(8,128)(2,1)}, bf16[120,2560]{1,0:T(8,128)(2,1)S(1)}, u32[]{:S(2)}, u32[]{:S(2)}) %collective-permute-start.21) | collective-permute-done | bytes 614432 | tf_op jit(solution)/shard_map/ppermute | solution.py:60
  257.0 3.6 %collective-permute-done.23.refs_3_ = bf16[120,2560]{1,0:T(8,128)(2,1)S(1)} collective-permute-done((bf16[120,2560]{1,0:T(8,128)(2,1)}, bf16[120,2560]{1,0:T(8,128)(2,1)S(1)}, u32[]{:S(2)}, u32[]{:S(2)}) %collective-permute-start.23) | collective-permute-done | bytes 614432 | tf_op jit(solution)/shard_map/ppermute | solution.py:60
  261.4 3.1 columns.1
  264.5 5.8 %collective-permute-start.28 = (bf16[120,640]{1,0:T(8,128)(2,1)}, bf16[120,640]{1,0:T(8,128)(2,1)S(1)}, u32[]{:S(2)}, u32[]{:S(2)}) collective-permute-start(bf16[120,640]{1,0:T(8,128)(2,1)} %get-tuple-element.123), channel_id=1, source_target_pairs={{0,64},{32,96},{64,0},{96,32},{1,65},{33,97},{65,1},{97,33},{2,66}... | collective-permute-start | bytes 460808 | tf_op jit(solution)/shard_map/ppermute | solution.py:60
  271.8 5.1 %last.1 = bf16[128,960]{1,0:T(8,128)(2,1)} custom-call(s32[40]{0:T(128)} %concatenate.18.ints, bf16[128,1024]{1,0:T(8,128)(2,1)} %get-tuple-element.106.dq_ref, bf16[16,128,640]{2,1,0:T(8,128)(2,1)} %copy-done, bf16[960,1664]{1,0:T(8,128)(2,1)} %get-tuple-element.78.w_ref, bf16[128,960]{1,0:T(8,128)(2,1)} %bitcast.59, f32[1,960]{1,0:T(1,128)} %get-tuple-element.194.gain_ref, ...), custom_call_target="tpu_custom_call" | custom-call | flops 1000 | bytes 1000 | tf_op jit(solution)/shard_map/last/pallas_call | solution.py:125
  278.8 3.2 %collective-permute-start.31 = (bf16[120,640]{1,0:T(8,128)(2,1)S(1)}, bf16[120,640]{1,0:T(8,128)(2,1)S(1)}, u32[]{:S(2)}, u32[]{:S(2)}) collective-permute-start(bf16[120,640]{1,0:T(8,128)(2,1)S(1)} %add_convert_fusion.2), channel_id=1, source_target_pairs={{0,16},{8,24},{16,0},{24,8},{1,17},{9,25},{17,1},{25,9},{2,18},{10... | collective-permute-start | bytes 460808 | tf_op jit(solution)/shard_map/ppermute | solution.py:60
  283.5 2.6 fold.3
  294.5 2.7 collective-permute-start.34
  305.4 2.9 finish.1
  308.3 4.2 %spread.1 = (f32[120,2560]{1,0:T(8,128)}, f32[120,2560]{1,0:T(8,128)}, f32[320,960]{1,0:T(8,128)}, f32[1,120]{1,0:T(1,128)}) custom-call(s32[40]{0:T(128)} %concatenate.18.ints, bf16[8,120,640]{2,1,0:T(8,128)(2,1)} %get-tuple-element.132.g_ref, bf16[320,960]{1,0:T(8,128)(2,1)} %get-tuple-element.184.d_ref, bf16[120,2560]{1,0:T(8,128)(2,1)} %wg_ref.1, ...), custom_call_target="tpu_custom_call" | custom-call | flops 1000 | bytes 1000 | tf_op jit(solution)/shard_map/spread/pallas_call | solution.py:125
  (185 shorter events, 75.3 us)
Async XLA Ops:
  7.2 61.4 %all-gather.6.cloned.1.call-start = ((), (), s32[]{:S(2)}) async-start(), calls=%async_computation.4 | async-start | bytes 4456448 | tf_op jit(solution)/shard_map/all_gather | solution.py:570
  9.1 99.7 %all-gather.4.cloned.1.call-start = ((), (), s32[]{:S(2)}) async-start(), calls=%async_computation.3 | async-start | bytes 2359296 | tf_op jit(solution)/shard_map/all_gather | solution.py:577
  14.5 29.6 %collective-permute-start.2 = (bf16[120,2624]{1,0:T(8,128)(2,1)S(1)}, bf16[120,2624]{1,0:T(8,128)(2,1)S(1)}, u32[]{:S(2)}, u32[]{:S(2)}) collective-permute-start(bf16[120,2624]{1,0:T(8,128)(2,1)S(1)} %concatenate.19.refs_0_), channel_id=1, source_target_pairs={{0,2},{2,4},{4,6},{6,0},{1,3},{3,5},{5,7},{7,1},{8,10},{10,12},{12... | collective-permute-start | bytes 1889288 | tf_op jit(solution)/shard_map/ppermute | solution.py:60
  16.5 27.6 %collective-permute-start.1 = (bf16[120,2624]{1,0:T(8,128)(2,1)S(1)}, bf16[120,2624]{1,0:T(8,128)(2,1)S(1)}, u32[]{:S(2)}, u32[]{:S(2)}) collective-permute-start(bf16[120,2624]{1,0:T(8,128)(2,1)S(1)} %concatenate.19.refs_0_), channel_id=1, source_target_pairs={{0,4},{2,6},{4,0},{6,2},{1,5},{3,7},{5,1},{7,3},{8,12},{10,14},{12... | collective-permute-start | bytes 1889288 | tf_op jit(solution)/shard_map/ppermute | solution.py:60
  17.6 29.9 %collective-permute-start = (bf16[120,2624]{1,0:T(8,128)(2,1)S(1)}, bf16[120,2624]{1,0:T(8,128)(2,1)}, u32[]{:S(2)}, u32[]{:S(2)}) collective-permute-start(bf16[120,2624]{1,0:T(8,128)(2,1)S(1)} %concatenate.19.refs_0_), channel_id=1, source_target_pairs={{0,6},{2,0},{4,2},{6,4},{1,7},{3,1},{5,3},{7,5},{8,14},{10,8},{12,... | collective-permute-start | bytes 1889288 | tf_op jit(solution)/shard_map/ppermute | solution.py:60
  20.2 29.0 %collective-permute-start.3 = (bf16[120,2624]{1,0:T(8,128)(2,1)S(1)}, bf16[120,2624]{1,0:T(8,128)(2,1)}, u32[]{:S(2)}, u32[]{:S(2)}) collective-permute-start(bf16[120,2624]{1,0:T(8,128)(2,1)S(1)} %concatenate.19.refs_0_), channel_id=1, source_target_pairs={{0,1},{1,0},{2,3},{3,2},{4,5},{5,4},{6,7},{7,6},{8,9},{9,8},{10,11... | collective-permute-start | bytes 1889288 | tf_op jit(solution)/shard_map/ppermute | solution.py:60
  57.9 49.5 %all-to-all-start = ((bf16[8,120,640]{2,1,0:T(8,128)(2,1)}), bf16[8,120,640]{2,1,0:T(8,128)(2,1)S(1)}, u32[]{:S(2)}, u32[]{:S(2)}) async-start(bf16[8,120,640]{2,1,0:T(8,128)(2,1)} %copy.106), calls=%async_computation | async-start | bytes 2457600 | tf_op jit(solution)/shard_map/all_to_all | solution.py:586
  92.6 10.9 %collective-permute-start.8 = (bf16[128,960]{1,0:T(8,128)(2,1)}, bf16[128,960]{1,0:T(8,128)(2,1)S(1)}, u32[]{:S(2)}, u32[]{:S(2)}) collective-permute-start(bf16[128,960]{1,0:T(8,128)(2,1)} %get-tuple-element.85.refs_0_), channel_id=1, source_target_pairs={{0,4},{2,6},{4,0},{6,2},{1,5},{3,7},{5,1},{7,3},{8,12},{10,14},{12... | collective-permute-start | bytes 737288 | tf_op jit(solution)/shard_map/ppermute | solution.py:60
  93.2 14.0 %collective-permute-start.7 = (bf16[128,960]{1,0:T(8,128)(2,1)}, bf16[128,960]{1,0:T(8,128)(2,1)S(1)}, u32[]{:S(2)}, u32[]{:S(2)}) collective-permute-start(bf16[128,960]{1,0:T(8,128)(2,1)} %get-tuple-element.85.refs_0_), channel_id=1, source_target_pairs={{0,6},{2,0},{4,2},{6,4},{1,7},{3,1},{5,3},{7,5},{8,14},{10,8},{12,... | collective-permute-start | bytes 737288 | tf_op jit(solution)/shard_map/ppermute | solution.py:60
  95.8 13.1 %collective-permute-start.10 = (bf16[128,960]{1,0:T(8,128)(2,1)}, bf16[128,960]{1,0:T(8,128)(2,1)S(1)}, u32[]{:S(2)}, u32[]{:S(2)}) collective-permute-start(bf16[128,960]{1,0:T(8,128)(2,1)} %get-tuple-element.85.refs_0_), channel_id=1, source_target_pairs={{0,1},{1,0},{2,3},{3,2},{4,5},{5,4},{6,7},{7,6},{8,9},{9,8},{10,11... | collective-permute-start | bytes 737288 | tf_op jit(solution)/shard_map/ppermute | solution.py:60
  124.5 21.7 %all-to-all-start.1 = ((bf16[8,120,640]{2,1,0:T(8,128)(2,1)}), bf16[8,120,640]{2,1,0:T(8,128)(2,1)S(1)}, u32[]{:S(2)}, u32[]{:S(2)}) async-start(bf16[8,120,640]{2,1,0:T(8,128)(2,1)} %get-tuple-element.95), calls=%async_computation.1 | async-start | bytes 2457600 | tf_op jit(solution)/shard_map/all_to_all | solution.py:597
  129.2 96.1 %all-reduce.7.cloned.1.call-start = ((), (), s32[]{:S(2)}) async-start(), calls=%async_computation.6 | async-start | bytes 3768320 | tf_op jit(solution)/shard_map/psum | solution.py:609
  132.8 17.0 %collective-permute-start.15 = (bf16[128,960]{1,0:T(8,128)(2,1)}, bf16[128,960]{1,0:T(8,128)(2,1)S(1)}, u32[]{:S(2)}, u32[]{:S(2)}) collective-permute-start(bf16[128,960]{1,0:T(8,128)(2,1)} %get-tuple-element.92), channel_id=1, source_target_pairs={{0,2},{2,4},{4,6},{6,0},{1,3},{3,5},{5,7},{7,1},{8,10},{10,12},{12... | collective-permute-start | bytes 737288 | tf_op jit(solution)/shard_map/ppermute | solution.py:60
  134.3 17.5 %collective-permute-start.16 = (bf16[128,960]{1,0:T(8,128)(2,1)}, bf16[128,960]{1,0:T(8,128)(2,1)S(1)}, u32[]{:S(2)}, u32[]{:S(2)}) collective-permute-start(bf16[128,960]{1,0:T(8,128)(2,1)} %get-tuple-element.93), channel_id=1, source_target_pairs={{0,4},{2,6},{4,0},{6,2},{1,5},{3,7},{5,1},{7,3},{8,12},{10,14},{12... | collective-permute-start | bytes 737288 | tf_op jit(solution)/shard_map/ppermute | solution.py:60
  134.9 21.3 %collective-permute-start.17 = (bf16[128,960]{1,0:T(8,128)(2,1)}, bf16[128,960]{1,0:T(8,128)(2,1)S(1)}, u32[]{:S(2)}, u32[]{:S(2)}) collective-permute-start(bf16[128,960]{1,0:T(8,128)(2,1)} %get-tuple-element.94), channel_id=1, source_target_pairs={{0,6},{2,0},{4,2},{6,4},{1,7},{3,1},{5,3},{7,5},{8,14},{10,8},{12,... | collective-permute-start | bytes 737288 | tf_op jit(solution)/shard_map/ppermute | solution.py:60
  182.9 87.4 %all-to-all-start.2 = ((bf16[16,128,640]{2,1,0:T(8,128)(2,1)}), bf16[16,128,640]{2,1,0:T(8,128)(2,1)S(1)}, u32[]{:S(2)}, u32[]{:S(2)}) async-start(bf16[16,128,640]{2,1,0:T(8,128)(2,1)} %bitcast.64), calls=%async_computation.2 | async-start | bytes 5242880 | tf_op jit(solution)/shard_map/all_to_all | solution.py:612
  190.5 117.9 %all-reduce.5.cloned.1.call-start = ((), (), s32[]{:S(2)}) async-start(), calls=%async_computation.5 | async-start | bytes 3768320 | tf_op jit(solution)/shard_map/psum | solution.py:616
  200.6 24.8 %collective-permute-start.19 = (bf16[4,120,1600]{2,1,0:T(8,128)(2,1)}, bf16[4,120,1600]{2,1,0:T(8,128)(2,1)}, u32[]{:S(2)}, u32[]{:S(2)}) collective-permute-start(bf16[4,120,1600]{2,1,0:T(8,128)(2,1)} %get-tuple-element.187), channel_id=1, source_target_pairs={{0,1},{1,0},{2,3},{3,2},{4,5},{5,4},{6,7},{7,6},{8,9},{9,8},{10,11... | collective-permute-start | bytes 4608008 | tf_op jit(solution)/shard_map/ppermute | solution.py:60
  200.6 24.8 %collective-permute-start.20 = (bf16[4,120,960]{2,1,0:T(8,128)(2,1)}, bf16[4,120,960]{2,1,0:T(8,128)(2,1)}, u32[]{:S(2)}, u32[]{:S(2)}) collective-permute-start(bf16[4,120,960]{2,1,0:T(8,128)(2,1)} %get-tuple-element.107), channel_id=1, source_target_pairs={{0,1},{1,0},{2,3},{3,2},{4,5},{5,4},{6,7},{7,6},{8,9},{9,8},{10,11... | collective-permute-start | bytes 2764808 | tf_op jit(solution)/shard_map/ppermute | solution.py:60
  229.8 27.1 %collective-permute-start.21 = (bf16[120,2560]{1,0:T(8,128)(2,1)}, bf16[120,2560]{1,0:T(8,128)(2,1)S(1)}, u32[]{:S(2)}, u32[]{:S(2)}) collective-permute-start(bf16[120,2560]{1,0:T(8,128)(2,1)} %get-tuple-element.110), channel_id=1, source_target_pairs={{0,2},{2,4},{4,6},{6,0},{1,3},{3,5},{5,7},{7,1},{8,10},{10,12},{12... | collective-permute-start | bytes 1843208 | tf_op jit(solution)/shard_map/ppermute | solution.py:60
  231.5 25.5 %collective-permute-start.22 = (bf16[120,2560]{1,0:T(8,128)(2,1)}, bf16[120,2560]{1,0:T(8,128)(2,1)S(1)}, u32[]{:S(2)}, u32[]{:S(2)}) collective-permute-start(bf16[120,2560]{1,0:T(8,128)(2,1)} %get-tuple-element.111), channel_id=1, source_target_pairs={{0,4},{2,6},{4,0},{6,2},{1,5},{3,7},{5,1},{7,3},{8,12},{10,14},{12... | collective-permute-start | bytes 1843208 | tf_op jit(solution)/shard_map/ppermute | solution.py:60
  232.6 27.9 %collective-permute-start.23 = (bf16[120,2560]{1,0:T(8,128)(2,1)}, bf16[120,2560]{1,0:T(8,128)(2,1)S(1)}, u32[]{:S(2)}, u32[]{:S(2)}) collective-permute-start(bf16[120,2560]{1,0:T(8,128)(2,1)} %get-tuple-element.112), channel_id=1, source_target_pairs={{0,6},{2,0},{4,2},{6,4},{1,7},{3,1},{5,3},{7,5},{8,14},{10,8},{12,... | collective-permute-start | bytes 1843208 | tf_op jit(solution)/shard_map/ppermute | solution.py:60
  235.3 48.2 %collective-permute-start.18 = (bf16[512,1024]{1,0:T(8,128)(2,1)}, bf16[512,1024]{1,0:T(8,128)(2,1)}, u32[]{:S(2)}, u32[]{:S(2)}) collective-permute-start(bf16[512,1024]{1,0:T(8,128)(2,1)} %get-tuple-element.101), channel_id=1, source_target_pairs={{0,1},{1,0},{2,3},{3,2},{4,5},{5,4},{6,7},{7,6},{8,9},{9,8},{10,11... | collective-permute-start | bytes 3145736 | tf_op jit(solution)/shard_map/ppermute | solution.py:60
  264.5 12.3 %collective-permute-start.27 = (bf16[120,640]{1,0:T(8,128)(2,1)}, bf16[120,640]{1,0:T(8,128)(2,1)S(1)}, u32[]{:S(2)}, u32[]{:S(2)}) collective-permute-start(bf16[120,640]{1,0:T(8,128)(2,1)} %get-tuple-element.122), channel_id=1, source_target_pairs={{0,32},{32,64},{64,96},{96,0},{1,33},{33,65},{65,97},{97,1},{2,34}... | collective-permute-start | bytes 460808 | tf_op jit(solution)/shard_map/ppermute | solution.py:60
  264.5 12.8 %collective-permute-start.28 = (bf16[120,640]{1,0:T(8,128)(2,1)}, bf16[120,640]{1,0:T(8,128)(2,1)S(1)}, u32[]{:S(2)}, u32[]{:S(2)}) collective-permute-start(bf16[120,640]{1,0:T(8,128)(2,1)} %get-tuple-element.123), channel_id=1, source_target_pairs={{0,64},{32,96},{64,0},{96,32},{1,65},{33,97},{65,1},{97,33},{2,66}... | collective-permute-start | bytes 460808 | tf_op jit(solution)/shard_map/ppermute | solution.py:60
  277.4 11.1 %collective-permute-start.32 = (bf16[120,640]{1,0:T(8,128)(2,1)S(1)}, bf16[120,640]{1,0:T(8,128)(2,1)S(1)}, u32[]{:S(2)}, u32[]{:S(2)}) collective-permute-start(bf16[120,640]{1,0:T(8,128)(2,1)S(1)} %add_convert_fusion.2), channel_id=1, source_target_pairs={{0,8},{8,16},{16,24},{24,0},{1,9},{9,17},{17,25},{25,1},{2,10},{10... | collective-permute-start | bytes 460808 | tf_op jit(solution)/shard_map/ppermute | solution.py:60
  278.8 14.0 %collective-permute-start.31 = (bf16[120,640]{1,0:T(8,128)(2,1)S(1)}, bf16[120,640]{1,0:T(8,128)(2,1)S(1)}, u32[]{:S(2)}, u32[]{:S(2)}) collective-permute-start(bf16[120,640]{1,0:T(8,128)(2,1)S(1)} %add_convert_fusion.2), channel_id=1, source_target_pairs={{0,16},{8,24},{16,0},{24,8},{1,17},{9,25},{17,1},{25,9},{2,18},{10... | collective-permute-start | bytes 460808 | tf_op jit(solution)/shard_map/ppermute | solution.py:60
  282.0 10.8 %collective-permute-start.30 = (bf16[120,640]{1,0:T(8,128)(2,1)S(1)}, bf16[120,640]{1,0:T(8,128)(2,1)S(1)}, u32[]{:S(2)}, u32[]{:S(2)}) collective-permute-start(bf16[120,640]{1,0:T(8,128)(2,1)S(1)} %add_convert_fusion.2), channel_id=1, source_target_pairs={{0,24},{8,0},{16,8},{24,16},{1,25},{9,1},{17,9},{25,17},{2,26},{10... | collective-permute-start | bytes 460808 | tf_op jit(solution)/shard_map/ppermute | solution.py:60
  286.0 11.1 %collective-permute-start.24 = (bf16[128,960]{1,0:T(8,128)(2,1)}, bf16[128,960]{1,0:T(8,128)(2,1)S(1)}, u32[]{:S(2)}, u32[]{:S(2)}) collective-permute-start(bf16[128,960]{1,0:T(8,128)(2,1)} %get-tuple-element.116), channel_id=1, source_target_pairs={{0,2},{2,4},{4,6},{6,0},{1,3},{3,5},{5,7},{7,1},{8,10},{10,12},{12... | collective-permute-start | bytes 737288 | tf_op jit(solution)/shard_map/ppermute | solution.py:60
  286.0 12.6 %collective-permute-start.25 = (bf16[128,960]{1,0:T(8,128)(2,1)}, bf16[128,960]{1,0:T(8,128)(2,1)S(1)}, u32[]{:S(2)}, u32[]{:S(2)}) collective-permute-start(bf16[128,960]{1,0:T(8,128)(2,1)} %get-tuple-element.117), channel_id=1, source_target_pairs={{0,4},{2,6},{4,0},{6,2},{1,5},{3,7},{5,1},{7,3},{8,12},{10,14},{12... | collective-permute-start | bytes 737288 | tf_op jit(solution)/shard_map/ppermute | solution.py:60
  288.5 11.5 %collective-permute-start.26 = (bf16[128,960]{1,0:T(8,128)(2,1)}, bf16[128,960]{1,0:T(8,128)(2,1)S(1)}, u32[]{:S(2)}, u32[]{:S(2)}) collective-permute-start(bf16[128,960]{1,0:T(8,128)(2,1)} %get-tuple-element.118), channel_id=1, source_target_pairs={{0,6},{2,0},{4,2},{6,4},{1,7},{3,1},{5,3},{7,5},{8,14},{10,8},{12,... | collective-permute-start | bytes 737288 | tf_op jit(solution)/shard_map/ppermute | solution.py:60
  292.9 9.9 %collective-permute-start.35 = (bf16[120,640]{1,0:T(8,128)(2,1)S(1)}, bf16[120,640]{1,0:T(8,128)(2,1)S(1)}, u32[]{:S(2)}, u32[]{:S(2)}) collective-permute-start(bf16[120,640]{1,0:T(8,128)(2,1)S(1)} %add_convert_fusion.1.p0), channel_id=1, source_target_pairs={{0,32},{32,64},{64,96},{96,0},{1,33},{33,65},{65,97},{97,1},{2,34}... | collective-permute-start | bytes 460808 | tf_op jit(solution)/shard_map/ppermute | solution.py:60
  (49 other events, 519.9 us)
Sparse Core Ops, SparseCore 0:
  10.7 53.4 all-gather.5
  65.9 25.2 all-gather.3
  147.4 77.8 all-reduce.6
  227.8 62.1 all-reduce.4
where the time goes:
time: 324 us; the launch traced here: 319 us
  waiting for transfers between devices  110 us (34%)
  Pallas kernels  89.1 us (28%)
  starting transfers between devices  62.5 us (19%)
  local copies, waits for them, and re-layouts  26.8 us (8%)
  between operations  14.4 us (4%)
  matrix products  9.66 us (3%)
  other arithmetic  7.06 us (2%)
    ppermute x36, waiting for transfers between devices, shift(): lax.ppermute(block, axis, [(i, (i - step) % size) for i in range(size)])  78.6 us
    pallas_call x12, Pallas kernels, call(): pl.pallas_call(kernel, in_specs=[in_smem()] + [in_vmem()] * (len(operands...  77.8 us
    ppermute x36, starting transfers between devices, shift(): lax.ppermute(block, axis, [(i, (i - step) % size) for i in range(size)])  44.5 us
    psum x1, waiting for transfers between devices, per_device(): g_gu, g_down = lax.psum((g_gu, g_down), 'x')  24.3 us
    unnamed x84, local copies, waits for them, and re-layouts  14.4 us
    pallas_call x1, Pallas kernels, qkv_call(): pl.pallas_call(qkv_kernel, grid=(length // tile,), in_specs=[in_smem(), t...  11.3 us
    dot_general x3, matrix products, left_dot(): lax.dot_general(left, right, (((0,), (0,)), ((), ())), preferred_element_...  9.66 us
    all_to_all x1, starting transfers between devices, per_device(): lax.all_to_all(dkv.reshape(pairs, rows, 2 * KD), CTX, 0, 0, tiled=True)  7.59 us
  transfers between devices with their start and end apart: 43, of which 17 were waited for; matrix products, arithmetic and copies ran while one was open for 11% of the time, Pallas kernels for 22%

commit v1 on v0

--- a/solution.py
+++ b/solution.py
@@ -609,12 +609,14 @@
     g_gu, g_down = lax.psum((g_gu, g_down), "x")
 
     dq, dkv = back_call(ints, q, kv, d_o, lse, delta, own_pos, start, cos, sin)
-    owners = lax.all_to_all(dkv.reshape(pairs, rows, 2 * KD), CTX, 0, 0, tiled=True)
     ha_own = lax.dynamic_slice_in_dim(ha_all, me * rows, rows, 0)
     g_kvq = jnp.concatenate([left_dot(ha_all, dkv), left_dot(ha_own, dq[:, :QD])], axis=1).astype(bf16)
     mine, its = by_core(g_kvq)
-    g_gu, g_down = lax.psum((after(g_gu, its), after(g_down, its)), "y")
-    z_parts = send_parts(turn_call(ints, mine, shift(its, "core", 1, 2), o_mine, after(o_recv, dq)), "z")
+    turned = turn_call(ints, mine, shift(its, "core", 1, 2), o_mine, after(o_recv, dq))
+    g_gu, g_down = after(g_gu, turned[0]), after(g_down, turned[0])
+    owners = lax.all_to_all(after(dkv, g_gu).reshape(pairs, rows, 2 * KD), CTX, 0, 0, tiled=True)
+    g_gu, g_down = lax.psum((g_gu, g_down), "y")
+    z_parts = send_parts(turned, "z")
     cut = columns_call(ints, z_parts)
     input_grad = last_call(ints, dq, after(owners, cut[0]), w_kvq, x_rows, gain_a, d_mid)
     x_parts = send_parts(cut, "x")
@@ -625,7 +627,7 @@
     g_key, g_value, g_query, g_out, g_gain_a = finish_call(
         ints, [low_sum] + [shift(low_sum, "x", k) for k in (1, 2, 3)], w_key, w_value, w_query, attn_gain[:, None]
     )
-    g_gate, g_up, g_down, g_gain_m = spread_call(ints, after(g_gu, input_grad, result), g_down, w_gate, w_up, mlp_gain[:, None])
+    g_gate, g_up, g_down, g_gain_m = spread_call(ints, after(g_gu, low_sum), g_down, w_gate, w_up, mlp_gain[:, None])
 
     return (
         result.reshape(1, 1, rows, width),

time: 324 us -> 307 us (0.948)
  waiting for transfers between devices: 110 us -> 94.8 us
    psum x1, waiting for transfers between devices: 24.3 us -> 2 us  [per_device(): g_gu, g_down = lax.psum((g_gu, g_down), 'x')]
    ppermute x36, waiting for transfers between devices: 78.6 us -> 82.7 us  [shift(): lax.ppermute(block, axis, [(i, (i - step) % size) for i in range(size)])]
    unnamed x84 -> x92, local copies, waits for them, and re-layouts: 14.4 us -> 15.9 us
  transfers between devices with their start and end apart: 43 -> 43, of which waited for: 17 -> 19; matrix products, arithmetic and copies ran while one was open for 11% -> 10% of each run, Pallas kernels for 22% -> 24%
where the time goes in v1:
time: 307 us; the launch traced here: 301 us
  waiting for transfers between devices  94.8 us (31%)
  Pallas kernels  89.7 us (29%)
  starting transfers between devices  59.6 us (19%)
  local copies, waits for them, and re-layouts  28 us (9%)
  between operations  14.4 us (5%)
  matrix products  7.61 us (2%)
  other arithmetic  6.68 us (2%)
    ppermute x36, waiting for transfers between devices, shift(): lax.ppermute(block, axis, [(i, (i - step) % size) for i in range(size)])  82.7 us
    pallas_call x12, Pallas kernels, call(): pl.pallas_call(kernel, in_specs=[in_smem()] + [in_vmem()] * (len(operands...  78.4 us
    ppermute x36, starting transfers between devices, shift(): lax.ppermute(block, axis, [(i, (i - step) % size) for i in range(size)])  43.7 us
    unnamed x92, local copies, waits for them, and re-layouts  15.9 us
    pallas_call x1, Pallas kernels, qkv_call(): pl.pallas_call(qkv_kernel, grid=(length // tile,), in_specs=[in_smem(), t...  11.3 us
    dot_general x3, matrix products, left_dot(): lax.dot_general(left, right, (((0,), (0,)), ((), ())), preferred_element_...  7.61 us
    all_to_all x1, waiting for transfers between devices, per_device(): g_gu = lax.all_to_all(g_gu, FSDP, 0, 0, tiled=True)  6.75 us
  transfers between devices with their start and end apart: 43, of which 19 were waited for; matrix products, arithmetic and copies ran while one was open for 10% of the time, Pallas kernels for 24%

profile of v1, /device:TPU:32, one launch (start us, length us, event | category | flops | bytes accessed | tf_op | source)
XLA Modules:
  0.0 300.8 jit_solution(15019900591503289498)
XLA Ops:
  20.2 23.9 %collective-permute-done.2.refs_3_ = bf16[120,2624]{1,0:T(8,128)(2,1)S(1)} collective-permute-done((bf16[120,2624]{1,0:T(8,128)(2,1)S(1)}, bf16[120,2624]{1,0:T(8,128)(2,1)S(1)}, u32[]{:S(2)}, u32[]{:S(2)}) %collective-permute-start.2) | collective-permute-done | bytes 629792 | tf_op jit(solution)/shard_map/ppermute | solution.py:60
  44.6 2.9 collective-permute-done.refs_1_
  50.0 5.5 %assemble.1 = (bf16[960,1664]{1,0:T(8,128)(2,1)}, bf16[960,960]{1,0:T(8,128)(2,1)}, f32[8,960]{1,0:T(8,128)}) custom-call(s32[40]{0:T(128)} %concatenate.18.ints, bf16[120,2624]{1,0:T(8,128)(2,1)} %copy-done.2, bf16[120,2624]{1,0:T(8,128)(2,1)} %collective-permute-done.refs_1_, bf16[120,2624]{1,0:T(8,128)(2,1)} %copy-done.15, bf16[120,2624]{1,0:T(8,128)(2,1)} %copy-done.14, ...), custom_call_target="tpu_custom_call" | custom-call | flops 1000 | bytes 1000 | tf_op jit(solution)/shard_map/assemble/pallas_call | solution.py:125
  57.9 5.6 %all-to-all-start = ((bf16[8,120,640]{2,1,0:T(8,128)(2,1)}), bf16[8,120,640]{2,1,0:T(8,128)(2,1)S(1)}, u32[]{:S(2)}, u32[]{:S(2)}) async-start(bf16[8,120,640]{2,1,0:T(8,128)(2,1)} %copy.106), calls=%async_computation | async-start | bytes 2457600 | tf_op jit(solution)/shard_map/all_to_all | solution.py:586
  68.5 11.3 %qkv.1 = (bf16[2048,960]{1,0:T(8,128)(2,1)}, bf16[2048,640]{1,0:T(8,128)(2,1)}, bf16[128,1024]{1,0:T(8,128)(2,1)}) custom-call(s32[40]{0:T(128)} %concatenate.18.ints, bf16[2048,960]{1,0:T(8,128)(2,1)} %bitcast.62, f32[2048,128]{1,0:T(8,128)} %constant.63.clone.cos_ref, f32[2048,128]{1,0:T(8,128)} %constant.64.clone.sin_ref, bf16[128,960]{1,0:T(8,128)(2,1)} %bitcast.58, ...), custom_call_target="tpu_custom_call" | custom-call | flops 1000 | bytes 1000 | tf_op jit(solution)/shard_map/qkv/pallas_call | solution.py:202
  80.5 10.6 %attend.1 = (bf16[128,960]{1,0:T(8,128)(2,1)}, f32[8,384]{1,0:T(8,128)}, f32[128,960]{1,0:T(8,128)}, bf16[128,960]{1,0:T(8,128)(2,1)}) custom-call(s32[40]{0:T(128)} %concatenate.18.ints, bf16[128,1024]{1,0:T(8,128)(2,1)} %get-tuple-element.81.q_ref, bf16[2048,640]{1,0:T(8,128)(2,1)} %get-tuple-element.82.kv_ref, s32[128,1]{1,0:T(8,128)} %copy.101.qpos_ref, ...), custom_call_target="tpu_custom_call" | custom-call | flops 1000 | bytes 1000 | tf_op jit(solution)/shard_map/attend/pallas_call | solution.py:125
  95.8 4.7 %collective-permute-done.9.refs_3_ = bf16[128,960]{1,0:T(8,128)(2,1)S(1)} collective-permute-done((bf16[128,960]{1,0:T(8,128)(2,1)}, bf16[128,960]{1,0:T(8,128)(2,1)S(1)}, u32[]{:S(2)}, u32[]{:S(2)}) %collective-permute-start.9) | collective-permute-done | bytes 245792 | tf_op jit(solution)/shard_map/ppermute | solution.py:60
  100.5 2.9 collective-permute-done.8.refs_2_
  103.4 3.8 %collective-permute-done.7.refs_1_ = bf16[128,960]{1,0:T(8,128)(2,1)S(1)} collective-permute-done((bf16[128,960]{1,0:T(8,128)(2,1)}, bf16[128,960]{1,0:T(8,128)(2,1)S(1)}, u32[]{:S(2)}, u32[]{:S(2)}) %collective-permute-start.7) | collective-permute-done | bytes 245792 | tf_op jit(solution)/shard_map/ppermute | solution.py:60
  109.9 14.1 %mlp.1 = (bf16[512,1024]{1,0:T(8,128)(2,1)}, bf16[512,1024]{1,0:T(8,128)(2,1)}, bf16[512,1024]{1,0:T(8,128)(2,1)}, bf16[512,1024]{1,0:T(8,128)(2,1)}, bf16[8,120...) custom-call(s32[40]{0:T(128)} %concatenate.18.ints, bf16[128,960]{1,0:T(8,128)(2,1)} %get-tuple-element.86.refs_0_, ...), custom_call_target="tpu_custom_call" | custom-call | flops 1000 | bytes 1000 | tf_op jit(solution)/shard_map/mlp/pallas_call | solution.py:125
  124.4 4.7 %all-to-all-start.1 = ((bf16[8,120,640]{2,1,0:T(8,128)(2,1)}), bf16[8,120,640]{2,1,0:T(8,128)(2,1)S(1)}, u32[]{:S(2)}, u32[]{:S(2)}) async-start(bf16[8,120,640]{2,1,0:T(8,128)(2,1)} %get-tuple-element.96), calls=%async_computation.1 | async-start | bytes 2457600 | tf_op jit(solution)/shard_map/all_to_all | solution.py:597
  134.8 2.8 collective-permute-start.17
  139.4 6.8 %all-to-all-done.1 = bf16[8,120,640]{2,1,0:T(8,128)(2,1)S(1)} async-done(((bf16[8,120,640]{2,1,0:T(8,128)(2,1)}), bf16[8,120,640]{2,1,0:T(8,128)(2,1)S(1)}, u32[]{:S(2)}, u32[]{:S(2)}) %all-to-all-start.1) | async-done | bytes 1228832 | tf_op jit(solution)/shard_map/all_to_all | solution.py:597
  151.7 4.5 %collective-permute-done.17.d3 = bf16[128,960]{1,0:T(8,128)(2,1)S(1)} collective-permute-done((bf16[128,960]{1,0:T(8,128)(2,1)}, bf16[128,960]{1,0:T(8,128)(2,1)S(1)}, u32[]{:S(2)}, u32[]{:S(2)}) %collective-permute-start.17) | collective-permute-done | bytes 245792 | tf_op jit(solution)/shard_map/ppermute | solution.py:60
  156.9 6.0 %middle.1 = (f32[128,960]{1,0:T(8,128)}, bf16[128,960]{1,0:T(8,128)(2,1)}, bf16[128,960]{1,0:T(8,128)(2,1)}, f32[8,384]{1,0:T(8,128)}) custom-call(s32[40]{0:T(128)} %concatenate.18.ints, bf16[128,960]{1,0:T(8,128)(2,1)} %get-tuple-element.92.d0, bf16[128,960]{1,0:T(8,128)(2,1)} %copy-done.22, bf16[128,960]{1,0:T(8,128)(2,1)} %copy-done.23, ...), custom_call_target="tpu_custom_call" | custom-call | flops 1000 | bytes 1000 | tf_op jit(solution)/shard_map/middle/pallas_call | solution.py:125
  165.7 17.4 %back.1 = (bf16[128,1024]{1,0:T(8,128)(2,1)}, bf16[2048,640]{1,0:T(8,128)(2,1)}) custom-call(s32[40]{0:T(128)} %concatenate.18.ints, bf16[128,1024]{1,0:T(8,128)(2,1)} %get-tuple-element.81.q_ref, bf16[2048,640]{1,0:T(8,128)(2,1)} %get-tuple-element.82.kv_ref, bf16[128,960]{1,0:T(8,128)(2,1)} %get-tuple-element.101.do_ref, ...), custom_call_target="tpu_custom_call" | custom-call | flops 1000 | bytes 1000 | tf_op jit(solution)/shard_map/back/pallas_call | solution.py:125
  183.0 5.3 %convolution_convert_fusion.2 = bf16[960,640]{1,0:T(8,128)(2,1)S(1)} fusion(bf16[2048,960]{1,0:T(8,128)(2,1)S(1)} %copy-done.37, bf16[2048,640]{1,0:T(8,128)(2,1)} %get-tuple-element.122), kind=kOutput, calls=%fused_computation.10 | convolution fusion | flops 2517196800 | bytes 7782400 | tf_op jit(solution)/shard_map/dot_general | solution.py:52
  191.1 4.3 %collective-permute-done.20.its2_ref = bf16[4,120,960]{2,1,0:T(8,128)(2,1)S(1)} collective-permute-done((bf16[4,120,960]{2,1,0:T(8,128)(2,1)S(1)}, bf16[4,120,960]{2,1,0:T(8,128)(2,1)S(1)}, u32[]{:S(2)}, u32[]{:S(2)}) %collective-permute-start.20) | collective-permute-done | bytes 921632 | tf_op jit(solution)/shard_map/ppermute | solution.py:60
  197.0 4.5 %turn.1 = (bf16[120,2560]{1,0:T(8,128)(2,1)}, bf16[120,2560]{1,0:T(8,128)(2,1)}, bf16[120,2560]{1,0:T(8,128)(2,1)}, bf16[120,2560]{1,0:T(8,128)(2,1)}) custom-call(s32[40]{0:T(128)} %concatenate.18.ints, bf16[4,120,1600]{2,1,0:T(8,128)(2,1)} %get-tuple-element.190.mine_ref, bf16[4,120,1600]{2,1,0:T(8,128)(2,1)} %copy-done.6, ...), custom_call_target="tpu_custom_call" | custom-call | flops 1000 | bytes 1000 | tf_op jit(solution)/shard_map/turn/pallas_call | solution.py:125
  203.5 5.5 %all-to-all-start.2 = ((bf16[16,128,640]{2,1,0:T(8,128)(2,1)}), bf16[16,128,640]{2,1,0:T(8,128)(2,1)S(1)}, u32[]{:S(2)}, u32[]{:S(2)}) async-start(bf16[16,128,640]{2,1,0:T(8,128)(2,1)} %bitcast.65), calls=%async_computation.2 | async-start | bytes 5242880 | tf_op jit(solution)/shard_map/all_to_all | solution.py:617
  214.5 12.1 %collective-permute-done.21.refs_1_ = bf16[120,2560]{1,0:T(8,128)(2,1)S(1)} collective-permute-done((bf16[120,2560]{1,0:T(8,128)(2,1)}, bf16[120,2560]{1,0:T(8,128)(2,1)S(1)}, u32[]{:S(2)}, u32[]{:S(2)}) %collective-permute-start.21) | collective-permute-done | bytes 614432 | tf_op jit(solution)/shard_map/ppermute | solution.py:60
  226.5 3.2 %collective-permute-done.22.refs_2_ = bf16[120,2560]{1,0:T(8,128)(2,1)S(1)} collective-permute-done((bf16[120,2560]{1,0:T(8,128)(2,1)}, bf16[120,2560]{1,0:T(8,128)(2,1)S(1)}, u32[]{:S(2)}, u32[]{:S(2)}) %collective-permute-start.22) | collective-permute-done | bytes 614432 | tf_op jit(solution)/shard_map/ppermute | solution.py:60
  229.7 11.4 %collective-permute-done.23.refs_3_ = bf16[120,2560]{1,0:T(8,128)(2,1)S(1)} collective-permute-done((bf16[120,2560]{1,0:T(8,128)(2,1)S(1)}, bf16[120,2560]{1,0:T(8,128)(2,1)S(1)}, u32[]{:S(2)}, u32[]{:S(2)}) %collective-permute-start.23) | collective-permute-done | bytes 614432 | tf_op jit(solution)/shard_map/ppermute | solution.py:60
  241.9 3.1 %columns.1 = (bf16[120,640]{1,0:T(8,128)(2,1)}, bf16[120,640]{1,0:T(8,128)(2,1)}, bf16[120,640]{1,0:T(8,128)(2,1)}, bf16[120,640]{1,0:T(8,128)(2,1)}) custom-call(s32[40]{0:T(128)} %concatenate.18.ints, bf16[120,2560]{1,0:T(8,128)(2,1)} %get-tuple-element.110.refs_0_, bf16[120,2560]{1,0:T(8,128)(2,1)} %copy-done.16, bf16[120,2560]{1,0:T(8,128)(2,1)} %copy-done.17, ...), custom_call_target="tpu_custom_call" | custom-call | flops 1000 | bytes 1000 | tf_op jit(solution)/shard_map/columns/pallas_call | solution.py:125
  246.7 2.7 collective-permute-start.28
  252.3 5.1 %last.1 = bf16[128,960]{1,0:T(8,128)(2,1)} custom-call(s32[40]{0:T(128)} %concatenate.18.ints, bf16[128,1024]{1,0:T(8,128)(2,1)} %get-tuple-element.107.dq_ref, bf16[16,128,640]{2,1,0:T(8,128)(2,1)} %copy-done, bf16[960,1664]{1,0:T(8,128)(2,1)} %get-tuple-element.79.w_ref, bf16[128,960]{1,0:T(8,128)(2,1)} %bitcast.60, f32[1,960]{1,0:T(1,128)} %get-tuple-element.196.gain_ref, ...), custom_call_target="tpu_custom_call" | custom-call | flops 1000 | bytes 1000 | tf_op jit(solution)/shard_map/last/pallas_call | solution.py:125
  259.0 2.7 collective-permute-start.31
  266.6 3.2 %collective-permute-start.25 = (bf16[128,960]{1,0:T(8,128)(2,1)}, bf16[128,960]{1,0:T(8,128)(2,1)S(1)}, u32[]{:S(2)}, u32[]{:S(2)}) collective-permute-start(bf16[128,960]{1,0:T(8,128)(2,1)} %get-tuple-element.118), channel_id=1, source_target_pairs={{0,4},{2,6},{4,0},{6,2},{1,5},{3,7},{5,1},{7,3},{8,12},{10,14},{12... | collective-permute-start | bytes 737288 | tf_op jit(solution)/shard_map/ppermute | solution.py:60
  277.2 2.7 collective-permute-done.26
  282.8 2.8 all-reduce.5.cloned.1.call-done
  285.6 4.2 %spread.1 = (f32[120,2560]{1,0:T(8,128)}, f32[120,2560]{1,0:T(8,128)}, f32[320,960]{1,0:T(8,128)}, f32[1,120]{1,0:T(1,128)}) custom-call(s32[40]{0:T(128)} %concatenate.18.ints, bf16[8,120,640]{2,1,0:T(8,128)(2,1)} %get-tuple-element.134.g_ref, bf16[320,960]{1,0:T(8,128)(2,1)} %get-tuple-element.186.d_ref, bf16[120,2560]{1,0:T(8,128)(2,1)} %wg_ref.1, ...), custom_call_target="tpu_custom_call" | custom-call | flops 1000 | bytes 1000 | tf_op jit(solution)/shard_map/spread/pallas_call | solution.py:125
  291.2 2.9 finish.1
  (193 shorter events, 83.5 us)
Async XLA Ops:
  7.2 61.3 %all-gather.6.cloned.1.call-start = ((), (), s32[]{:S(2)}) async-start(), calls=%async_computation.4 | async-start | bytes 4456448 | tf_op jit(solution)/shard_map/all_gather | solution.py:570
  9.1 99.7 %all-gather.4.cloned.1.call-start = ((), (), s32[]{:S(2)}) async-start(), calls=%async_computation.3 | async-start | bytes 2359296 | tf_op jit(solution)/shard_map/all_gather | solution.py:577
  14.5 29.6 %collective-permute-start.2 = (bf16[120,2624]{1,0:T(8,128)(2,1)S(1)}, bf16[120,2624]{1,0:T(8,128)(2,1)S(1)}, u32[]{:S(2)}, u32[]{:S(2)}) collective-permute-start(bf16[120,2624]{1,0:T(8,128)(2,1)S(1)} %concatenate.19.refs_0_), channel_id=1, source_target_pairs={{0,2},{2,4},{4,6},{6,0},{1,3},{3,5},{5,7},{7,1},{8,10},{10,12},{12... | collective-permute-start | bytes 1889288 | tf_op jit(solution)/shard_map/ppermute | solution.py:60
  16.5 27.6 %collective-permute-start.1 = (bf16[120,2624]{1,0:T(8,128)(2,1)S(1)}, bf16[120,2624]{1,0:T(8,128)(2,1)S(1)}, u32[]{:S(2)}, u32[]{:S(2)}) collective-permute-start(bf16[120,2624]{1,0:T(8,128)(2,1)S(1)} %concatenate.19.refs_0_), channel_id=1, source_target_pairs={{0,4},{2,6},{4,0},{6,2},{1,5},{3,7},{5,1},{7,3},{8,12},{10,14},{12... | collective-permute-start | bytes 1889288 | tf_op jit(solution)/shard_map/ppermute | solution.py:60
  17.6 29.9 %collective-permute-start = (bf16[120,2624]{1,0:T(8,128)(2,1)S(1)}, bf16[120,2624]{1,0:T(8,128)(2,1)}, u32[]{:S(2)}, u32[]{:S(2)}) collective-permute-start(bf16[120,2624]{1,0:T(8,128)(2,1)S(1)} %concatenate.19.refs_0_), channel_id=1, source_target_pairs={{0,6},{2,0},{4,2},{6,4},{1,7},{3,1},{5,3},{7,5},{8,14},{10,8},{12,... | collective-permute-start | bytes 1889288 | tf_op jit(solution)/shard_map/ppermute | solution.py:60
  20.2 29.0 %collective-permute-start.3 = (bf16[120,2624]{1,0:T(8,128)(2,1)S(1)}, bf16[120,2624]{1,0:T(8,128)(2,1)}, u32[]{:S(2)}, u32[]{:S(2)}) collective-permute-start(bf16[120,2624]{1,0:T(8,128)(2,1)S(1)} %concatenate.19.refs_0_), channel_id=1, source_target_pairs={{0,1},{1,0},{2,3},{3,2},{4,5},{5,4},{6,7},{7,6},{8,9},{9,8},{10,11... | collective-permute-start | bytes 1889288 | tf_op jit(solution)/shard_map/ppermute | solution.py:60
  57.9 49.5 %all-to-all-start = ((bf16[8,120,640]{2,1,0:T(8,128)(2,1)}), bf16[8,120,640]{2,1,0:T(8,128)(2,1)S(1)}, u32[]{:S(2)}, u32[]{:S(2)}) async-start(bf16[8,120,640]{2,1,0:T(8,128)(2,1)} %copy.106), calls=%async_computation | async-start | bytes 2457600 | tf_op jit(solution)/shard_map/all_to_all | solution.py:586
  92.5 10.9 %collective-permute-start.8 = (bf16[128,960]{1,0:T(8,128)(2,1)}, bf16[128,960]{1,0:T(8,128)(2,1)S(1)}, u32[]{:S(2)}, u32[]{:S(2)}) collective-permute-start(bf16[128,960]{1,0:T(8,128)(2,1)} %get-tuple-element.86.refs_0_), channel_id=1, source_target_pairs={{0,4},{2,6},{4,0},{6,2},{1,5},{3,7},{5,1},{7,3},{8,12},{10,14},{12... | collective-permute-start | bytes 737288 | tf_op jit(solution)/shard_map/ppermute | solution.py:60
  93.2 14.0 %collective-permute-start.7 = (bf16[128,960]{1,0:T(8,128)(2,1)}, bf16[128,960]{1,0:T(8,128)(2,1)S(1)}, u32[]{:S(2)}, u32[]{:S(2)}) collective-permute-start(bf16[128,960]{1,0:T(8,128)(2,1)} %get-tuple-element.86.refs_0_), channel_id=1, source_target_pairs={{0,6},{2,0},{4,2},{6,4},{1,7},{3,1},{5,3},{7,5},{8,14},{10,8},{12,... | collective-permute-start | bytes 737288 | tf_op jit(solution)/shard_map/ppermute | solution.py:60
  95.8 13.1 %collective-permute-start.10 = (bf16[128,960]{1,0:T(8,128)(2,1)}, bf16[128,960]{1,0:T(8,128)(2,1)S(1)}, u32[]{:S(2)}, u32[]{:S(2)}) collective-permute-start(bf16[128,960]{1,0:T(8,128)(2,1)} %get-tuple-element.86.refs_0_), channel_id=1, source_target_pairs={{0,1},{1,0},{2,3},{3,2},{4,5},{5,4},{6,7},{7,6},{8,9},{9,8},{10,11... | collective-permute-start | bytes 737288 | tf_op jit(solution)/shard_map/ppermute | solution.py:60
  124.4 21.7 %all-to-all-start.1 = ((bf16[8,120,640]{2,1,0:T(8,128)(2,1)}), bf16[8,120,640]{2,1,0:T(8,128)(2,1)S(1)}, u32[]{:S(2)}, u32[]{:S(2)}) async-start(bf16[8,120,640]{2,1,0:T(8,128)(2,1)} %get-tuple-element.96), calls=%async_computation.1 | async-start | bytes 2457600 | tf_op jit(solution)/shard_map/all_to_all | solution.py:597
  129.1 74.3 %all-reduce.7.cloned.1.call-start = ((), (), s32[]{:S(2)}) async-start(), calls=%async_computation.6 | async-start | bytes 3768320 | tf_op jit(solution)/shard_map/psum | solution.py:609
  132.7 17.0 %collective-permute-start.15 = (bf16[128,960]{1,0:T(8,128)(2,1)}, bf16[128,960]{1,0:T(8,128)(2,1)S(1)}, u32[]{:S(2)}, u32[]{:S(2)}) collective-permute-start(bf16[128,960]{1,0:T(8,128)(2,1)} %get-tuple-element.93), channel_id=1, source_target_pairs={{0,2},{2,4},{4,6},{6,0},{1,3},{3,5},{5,7},{7,1},{8,10},{10,12},{12... | collective-permute-start | bytes 737288 | tf_op jit(solution)/shard_map/ppermute | solution.py:60
  134.2 17.6 %collective-permute-start.16 = (bf16[128,960]{1,0:T(8,128)(2,1)}, bf16[128,960]{1,0:T(8,128)(2,1)S(1)}, u32[]{:S(2)}, u32[]{:S(2)}) collective-permute-start(bf16[128,960]{1,0:T(8,128)(2,1)} %get-tuple-element.94), channel_id=1, source_target_pairs={{0,4},{2,6},{4,0},{6,2},{1,5},{3,7},{5,1},{7,3},{8,12},{10,14},{12... | collective-permute-start | bytes 737288 | tf_op jit(solution)/shard_map/ppermute | solution.py:60
  134.8 21.4 %collective-permute-start.17 = (bf16[128,960]{1,0:T(8,128)(2,1)}, bf16[128,960]{1,0:T(8,128)(2,1)S(1)}, u32[]{:S(2)}, u32[]{:S(2)}) collective-permute-start(bf16[128,960]{1,0:T(8,128)(2,1)} %get-tuple-element.95), channel_id=1, source_target_pairs={{0,6},{2,0},{4,2},{6,4},{1,7},{3,1},{5,3},{7,5},{8,14},{10,8},{12,... | collective-permute-start | bytes 737288 | tf_op jit(solution)/shard_map/ppermute | solution.py:60
  203.5 47.3 %all-to-all-start.2 = ((bf16[16,128,640]{2,1,0:T(8,128)(2,1)}), bf16[16,128,640]{2,1,0:T(8,128)(2,1)S(1)}, u32[]{:S(2)}, u32[]{:S(2)}) async-start(bf16[16,128,640]{2,1,0:T(8,128)(2,1)} %bitcast.65), calls=%async_computation.2 | async-start | bytes 5242880 | tf_op jit(solution)/shard_map/all_to_all | solution.py:617
  209.0 76.7 %all-reduce.5.cloned.1.call-start = ((), (), s32[]{:S(2)}) async-start(), calls=%async_computation.5 | async-start | bytes 3768320 | tf_op jit(solution)/shard_map/psum | solution.py:618
  209.5 17.0 %collective-permute-start.21 = (bf16[120,2560]{1,0:T(8,128)(2,1)}, bf16[120,2560]{1,0:T(8,128)(2,1)S(1)}, u32[]{:S(2)}, u32[]{:S(2)}) collective-permute-start(bf16[120,2560]{1,0:T(8,128)(2,1)} %get-tuple-element.111), channel_id=1, source_target_pairs={{0,2},{2,4},{4,6},{6,0},{1,3},{3,5},{5,7},{7,1},{8,10},{10,12},{12... | collective-permute-start | bytes 1843208 | tf_op jit(solution)/shard_map/ppermute | solution.py:60
  211.2 18.5 %collective-permute-start.22 = (bf16[120,2560]{1,0:T(8,128)(2,1)}, bf16[120,2560]{1,0:T(8,128)(2,1)S(1)}, u32[]{:S(2)}, u32[]{:S(2)}) collective-permute-start(bf16[120,2560]{1,0:T(8,128)(2,1)} %get-tuple-element.112), channel_id=1, source_target_pairs={{0,4},{2,6},{4,0},{6,2},{1,5},{3,7},{5,1},{7,3},{8,12},{10,14},{12... | collective-permute-start | bytes 1843208 | tf_op jit(solution)/shard_map/ppermute | solution.py:60
  213.7 27.4 %collective-permute-start.23 = (bf16[120,2560]{1,0:T(8,128)(2,1)S(1)}, bf16[120,2560]{1,0:T(8,128)(2,1)S(1)}, u32[]{:S(2)}, u32[]{:S(2)}) collective-permute-start(bf16[120,2560]{1,0:T(8,128)(2,1)S(1)} %copy-done.41), channel_id=1, source_target_pairs={{0,6},{2,0},{4,2},{6,4},{1,7},{3,1},{5,3},{7,5},{8,14},{10,8},{12,... | collective-permute-start | bytes 1843208 | tf_op jit(solution)/shard_map/ppermute | solution.py:60
  214.5 48.7 %collective-permute-start.18 = (bf16[512,1024]{1,0:T(8,128)(2,1)}, bf16[512,1024]{1,0:T(8,128)(2,1)}, u32[]{:S(2)}, u32[]{:S(2)}) collective-permute-start(bf16[512,1024]{1,0:T(8,128)(2,1)} %get-tuple-element.102), channel_id=1, source_target_pairs={{0,1},{1,0},{2,3},{3,2},{4,5},{5,4},{6,7},{7,6},{8,9},{9,8},{10,11... | collective-permute-start | bytes 3145736 | tf_op jit(solution)/shard_map/ppermute | solution.py:60
  245.0 12.4 %collective-permute-start.27 = (bf16[120,640]{1,0:T(8,128)(2,1)}, bf16[120,640]{1,0:T(8,128)(2,1)S(1)}, u32[]{:S(2)}, u32[]{:S(2)}) collective-permute-start(bf16[120,640]{1,0:T(8,128)(2,1)} %get-tuple-element.126), channel_id=1, source_target_pairs={{0,32},{32,64},{64,96},{96,0},{1,33},{33,65},{65,97},{97,1},{2,34}... | collective-permute-start | bytes 460808 | tf_op jit(solution)/shard_map/ppermute | solution.py:60
  246.7 10.7 %collective-permute-start.28 = (bf16[120,640]{1,0:T(8,128)(2,1)}, bf16[120,640]{1,0:T(8,128)(2,1)S(1)}, u32[]{:S(2)}, u32[]{:S(2)}) collective-permute-start(bf16[120,640]{1,0:T(8,128)(2,1)} %get-tuple-element.127), channel_id=1, source_target_pairs={{0,64},{32,96},{64,0},{96,32},{1,65},{33,97},{65,1},{97,33},{2,66}... | collective-permute-start | bytes 460808 | tf_op jit(solution)/shard_map/ppermute | solution.py:60
  257.5 12.3 %collective-permute-start.32 = (bf16[120,640]{1,0:T(8,128)(2,1)S(1)}, bf16[120,640]{1,0:T(8,128)(2,1)S(1)}, u32[]{:S(2)}, u32[]{:S(2)}) collective-permute-start(bf16[120,640]{1,0:T(8,128)(2,1)S(1)} %add_convert_fusion.2), channel_id=1, source_target_pairs={{0,8},{8,16},{16,24},{24,0},{1,9},{9,17},{17,25},{25,1},{2,10},{10... | collective-permute-start | bytes 460808 | tf_op jit(solution)/shard_map/ppermute | solution.py:60
  259.0 12.3 %collective-permute-start.31 = (bf16[120,640]{1,0:T(8,128)(2,1)S(1)}, bf16[120,640]{1,0:T(8,128)(2,1)S(1)}, u32[]{:S(2)}, u32[]{:S(2)}) collective-permute-start(bf16[120,640]{1,0:T(8,128)(2,1)S(1)} %add_convert_fusion.2), channel_id=1, source_target_pairs={{0,16},{8,24},{16,0},{24,8},{1,17},{9,25},{17,1},{25,9},{2,18},{10... | collective-permute-start | bytes 460808 | tf_op jit(solution)/shard_map/ppermute | solution.py:60
  261.7 9.6 %collective-permute-start.30 = (bf16[120,640]{1,0:T(8,128)(2,1)S(1)}, bf16[120,640]{1,0:T(8,128)(2,1)S(1)}, u32[]{:S(2)}, u32[]{:S(2)}) collective-permute-start(bf16[120,640]{1,0:T(8,128)(2,1)S(1)} %add_convert_fusion.2), channel_id=1, source_target_pairs={{0,24},{8,0},{16,8},{24,16},{1,25},{9,1},{17,9},{25,17},{2,26},{10... | collective-permute-start | bytes 460808 | tf_op jit(solution)/shard_map/ppermute | solution.py:60
  265.8 9.6 %collective-permute-start.24 = (bf16[128,960]{1,0:T(8,128)(2,1)}, bf16[128,960]{1,0:T(8,128)(2,1)S(1)}, u32[]{:S(2)}, u32[]{:S(2)}) collective-permute-start(bf16[128,960]{1,0:T(8,128)(2,1)} %get-tuple-element.117), channel_id=1, source_target_pairs={{0,2},{2,4},{4,6},{6,0},{1,3},{3,5},{5,7},{7,1},{8,10},{10,12},{12... | collective-permute-start | bytes 737288 | tf_op jit(solution)/shard_map/ppermute | solution.py:60
  266.6 10.7 %collective-permute-start.25 = (bf16[128,960]{1,0:T(8,128)(2,1)}, bf16[128,960]{1,0:T(8,128)(2,1)S(1)}, u32[]{:S(2)}, u32[]{:S(2)}) collective-permute-start(bf16[128,960]{1,0:T(8,128)(2,1)} %get-tuple-element.118), channel_id=1, source_target_pairs={{0,4},{2,6},{4,0},{6,2},{1,5},{3,7},{5,1},{7,3},{8,12},{10,14},{12... | collective-permute-start | bytes 737288 | tf_op jit(solution)/shard_map/ppermute | solution.py:60
  269.8 10.2 %collective-permute-start.26 = (bf16[128,960]{1,0:T(8,128)(2,1)}, bf16[128,960]{1,0:T(8,128)(2,1)S(1)}, u32[]{:S(2)}, u32[]{:S(2)}) collective-permute-start(bf16[128,960]{1,0:T(8,128)(2,1)} %get-tuple-element.119), channel_id=1, source_target_pairs={{0,6},{2,0},{4,2},{6,4},{1,7},{3,1},{5,3},{7,5},{8,14},{10,8},{12,... | collective-permute-start | bytes 737288 | tf_op jit(solution)/shard_map/ppermute | solution.py:60
  271.4 18.3 %collective-permute-start.35 = (bf16[120,640]{1,0:T(8,128)(2,1)S(1)}, bf16[120,640]{1,0:T(8,128)(2,1)S(1)}, u32[]{:S(2)}, u32[]{:S(2)}) collective-permute-start(bf16[120,640]{1,0:T(8,128)(2,1)S(1)} %add_convert_fusion.1.p0), channel_id=1, source_target_pairs={{0,32},{32,64},{64,96},{96,0},{1,33},{33,65},{65,97},{97,1},{2,34}... | collective-permute-start | bytes 460808 | tf_op jit(solution)/shard_map/ppermute | solution.py:60
  272.1 17.7 %collective-permute-start.34 = (bf16[120,640]{1,0:T(8,128)(2,1)S(1)}, bf16[120,640]{1,0:T(8,128)(2,1)S(1)}, u32[]{:S(2)}, u32[]{:S(2)}) collective-permute-start(bf16[120,640]{1,0:T(8,128)(2,1)S(1)} %add_convert_fusion.1.p0), channel_id=1, source_target_pairs={{0,64},{32,96},{64,0},{96,32},{1,65},{33,97},{65,1},{97,33},{2,66}... | collective-permute-start | bytes 460808 | tf_op jit(solution)/shard_map/ppermute | solution.py:60
  275.4 14.5 %collective-permute-start.33 = (bf16[120,640]{1,0:T(8,128)(2,1)S(1)}, bf16[120,640]{1,0:T(8,128)(2,1)S(1)}, u32[]{:S(2)}, u32[]{:S(2)}) collective-permute-start(bf16[120,640]{1,0:T(8,128)(2,1)S(1)} %add_convert_fusion.1.p0), channel_id=1, source_target_pairs={{0,96},{32,0},{64,32},{96,64},{1,97},{33,1},{65,33},{97,65},{2,98}... | collective-permute-start | bytes 460808 | tf_op jit(solution)/shard_map/ppermute | solution.py:60
  (53 other events, 567.4 us)
Sparse Core Ops, SparseCore 0:
  10.7 53.4 all-gather.5
  65.9 25.2 all-gather.3
  147.3 56.1 all-reduce.6
  212.1 73.5 all-reduce.4

commit v2 on v1

--- a/solution.py
+++ b/solution.py
@@ -617,12 +617,14 @@
     owners = lax.all_to_all(after(dkv, g_gu).reshape(pairs, rows, 2 * KD), CTX, 0, 0, tiled=True)
     g_gu, g_down = lax.psum((g_gu, g_down), "y")
     z_parts = send_parts(turned, "z")
+    out_parts = fold_call(ints, out, after(out_recv, turned[0]), width)
+    z_parts[0] = after(z_parts[0], out_parts[0])
     cut = columns_call(ints, z_parts)
     input_grad = last_call(ints, dq, after(owners, cut[0]), w_kvq, x_rows, gain_a, d_mid)
     x_parts = send_parts(cut, "x")
     low_sum = add_parts([after(x_parts[0], input_grad)] + x_parts[1:]).astype(bf16)
     low_sum = add_parts([low_sum] + [shift(low_sum, "y", k) for k in (1, 2, 3)]).astype(bf16)
-    out_parts = fold_call(ints, out, after(out_recv, cut[0]), width)
+    *out_parts, _ = lax.optimization_barrier((*out_parts, cut[0]))
     result = (mid + add_parts(send_parts(out_parts, "z"))).astype(bf16)
     g_key, g_value, g_query, g_out, g_gain_a = finish_call(
         ints, [low_sum] + [shift(low_sum, "x", k) for k in (1, 2, 3)], w_key, w_value, w_query, attn_gain[:, None]

time: 307 us -> 307 us (level)
    unnamed x92 -> x100, local copies, waits for them, and re-layouts: 15.9 us -> 16.1 us
  transfers between devices with their start and end apart: 43 -> 43, of which waited for: 19 -> 20; matrix products, arithmetic and copies ran while one was open for 10% -> 10% of each run, Pallas kernels for 24% -> 24%
where the time goes in v2:
time: 307 us; the launch traced here: 301 us
  waiting for transfers between devices  96 us (31%)
  Pallas kernels  89.9 us (29%)
  starting transfers between devices  59.1 us (19%)
  local copies, waits for them, and re-layouts  28.2 us (9%)
  between operations  14.5 us (5%)
  matrix products  7.62 us (2%)
  other arithmetic  5.62 us (2%)
    ppermute x36, waiting for transfers between devices, shift(): lax.ppermute(block, axis, [(i, (i - step) % size) for i in range(size)])  81.1 us
    pallas_call x12, Pallas kernels, call(): pl.pallas_call(kernel, in_specs=[in_smem()] + [in_vmem()] * (len(operands...  78.5 us
    ppermute x36, starting transfers between devices, shift(): lax.ppermute(block, axis, [(i, (i - step) % size) for i in range(size)])  43.2 us
    unnamed x100, local copies, waits for them, and re-layouts  16.1 us
    pallas_call x1, Pallas kernels, qkv_call(): pl.pallas_call(qkv_kernel, grid=(length // tile,), in_specs=[in_smem(), t...  11.3 us
    dot_general x3, matrix products, left_dot(): lax.dot_general(left, right, (((0,), (0,)), ((), ())), preferred_element_...  7.62 us
    all_to_all x1, waiting for transfers between devices, per_device(): g_gu = lax.all_to_all(g_gu, FSDP, 0, 0, tiled=True)  6.73 us
  transfers between devices with their start and end apart: 43, of which 20 were waited for; matrix products, arithmetic and copies ran while one was open for 10% of the time, Pallas kernels for 24%

profile of v2, /device:TPU:32, one launch (start us, length us, event | category | flops | bytes accessed | tf_op | source)
XLA Modules:
  0.0 300.9 jit_solution(17904156743665961645)
XLA Ops:
  20.2 23.9 %collective-permute-done.2.refs_3_ = bf16[120,2624]{1,0:T(8,128)(2,1)S(1)} collective-permute-done((bf16[120,2624]{1,0:T(8,128)(2,1)S(1)}, bf16[120,2624]{1,0:T(8,128)(2,1)S(1)}, u32[]{:S(2)}, u32[]{:S(2)}) %collective-permute-start.2) | collective-permute-done | bytes 629792 | tf_op jit(solution)/shard_map/ppermute | solution.py:60
  44.6 2.9 collective-permute-done.refs_1_
  50.0 5.5 %assemble.1 = (bf16[960,1664]{1,0:T(8,128)(2,1)}, bf16[960,960]{1,0:T(8,128)(2,1)}, f32[8,960]{1,0:T(8,128)}) custom-call(s32[40]{0:T(128)} %concatenate.18.ints, bf16[120,2624]{1,0:T(8,128)(2,1)} %copy-done.2, bf16[120,2624]{1,0:T(8,128)(2,1)} %collective-permute-done.refs_1_, bf16[120,2624]{1,0:T(8,128)(2,1)} %copy-done.15, bf16[120,2624]{1,0:T(8,128)(2,1)} %copy-done.14, ...), custom_call_target="tpu_custom_call" | custom-call | flops 1000 | bytes 1000 | tf_op jit(solution)/shard_map/assemble/pallas_call | solution.py:125
  57.9 5.6 %all-to-all-start = ((bf16[8,120,640]{2,1,0:T(8,128)(2,1)}), bf16[8,120,640]{2,1,0:T(8,128)(2,1)S(1)}, u32[]{:S(2)}, u32[]{:S(2)}) async-start(bf16[8,120,640]{2,1,0:T(8,128)(2,1)} %copy.106), calls=%async_computation | async-start | bytes 2457600 | tf_op jit(solution)/shard_map/all_to_all | solution.py:586
  68.6 11.3 %qkv.1 = (bf16[2048,960]{1,0:T(8,128)(2,1)}, bf16[2048,640]{1,0:T(8,128)(2,1)}, bf16[128,1024]{1,0:T(8,128)(2,1)}) custom-call(s32[40]{0:T(128)} %concatenate.18.ints, bf16[2048,960]{1,0:T(8,128)(2,1)} %bitcast.62, f32[2048,128]{1,0:T(8,128)} %constant.63.clone.cos_ref, f32[2048,128]{1,0:T(8,128)} %constant.64.clone.sin_ref, bf16[128,960]{1,0:T(8,128)(2,1)} %bitcast.58, ...), custom_call_target="tpu_custom_call" | custom-call | flops 1000 | bytes 1000 | tf_op jit(solution)/shard_map/qkv/pallas_call | solution.py:202
  80.7 10.6 %attend.1 = (bf16[128,960]{1,0:T(8,128)(2,1)}, f32[8,384]{1,0:T(8,128)}, f32[128,960]{1,0:T(8,128)}, bf16[128,960]{1,0:T(8,128)(2,1)}) custom-call(s32[40]{0:T(128)} %concatenate.18.ints, bf16[128,1024]{1,0:T(8,128)(2,1)} %get-tuple-element.86.q_ref, bf16[2048,640]{1,0:T(8,128)(2,1)} %get-tuple-element.87.kv_ref, s32[128,1]{1,0:T(8,128)} %copy.101.qpos_ref, ...), custom_call_target="tpu_custom_call" | custom-call | flops 1000 | bytes 1000 | tf_op jit(solution)/shard_map/attend/pallas_call | solution.py:125
  95.9 4.8 %collective-permute-done.9.refs_3_ = bf16[128,960]{1,0:T(8,128)(2,1)S(1)} collective-permute-done((bf16[128,960]{1,0:T(8,128)(2,1)}, bf16[128,960]{1,0:T(8,128)(2,1)S(1)}, u32[]{:S(2)}, u32[]{:S(2)}) %collective-permute-start.9) | collective-permute-done | bytes 245792 | tf_op jit(solution)/shard_map/ppermute | solution.py:60
  100.6 2.9 collective-permute-done.8.refs_2_
  103.6 3.7 %collective-permute-done.7.refs_1_ = bf16[128,960]{1,0:T(8,128)(2,1)S(1)} collective-permute-done((bf16[128,960]{1,0:T(8,128)(2,1)}, bf16[128,960]{1,0:T(8,128)(2,1)S(1)}, u32[]{:S(2)}, u32[]{:S(2)}) %collective-permute-start.7) | collective-permute-done | bytes 245792 | tf_op jit(solution)/shard_map/ppermute | solution.py:60
  110.0 14.1 %mlp.1 = (bf16[512,1024]{1,0:T(8,128)(2,1)}, bf16[512,1024]{1,0:T(8,128)(2,1)}, bf16[512,1024]{1,0:T(8,128)(2,1)}, bf16[512,1024]{1,0:T(8,128)(2,1)}, bf16[8,120...) custom-call(s32[40]{0:T(128)} %concatenate.18.ints, bf16[128,960]{1,0:T(8,128)(2,1)} %get-tuple-element.91.refs_0_, ...), custom_call_target="tpu_custom_call" | custom-call | flops 1000 | bytes 1000 | tf_op jit(solution)/shard_map/mlp/pallas_call | solution.py:125
  124.5 4.7 %all-to-all-start.1 = ((bf16[8,120,640]{2,1,0:T(8,128)(2,1)}), bf16[8,120,640]{2,1,0:T(8,128)(2,1)S(1)}, u32[]{:S(2)}, u32[]{:S(2)}) async-start(bf16[8,120,640]{2,1,0:T(8,128)(2,1)} %get-tuple-element.101), calls=%async_computation.1 | async-start | bytes 2457600 | tf_op jit(solution)/shard_map/all_to_all | solution.py:597
  135.0 2.8 collective-permute-start.17
  139.6 6.7 %all-to-all-done.1 = bf16[8,120,640]{2,1,0:T(8,128)(2,1)S(1)} async-done(((bf16[8,120,640]{2,1,0:T(8,128)(2,1)}), bf16[8,120,640]{2,1,0:T(8,128)(2,1)S(1)}, u32[]{:S(2)}, u32[]{:S(2)}) %all-to-all-start.1) | async-done | bytes 1228832 | tf_op jit(solution)/shard_map/all_to_all | solution.py:597
  151.9 4.5 %collective-permute-done.17.d3 = bf16[128,960]{1,0:T(8,128)(2,1)S(1)} collective-permute-done((bf16[128,960]{1,0:T(8,128)(2,1)}, bf16[128,960]{1,0:T(8,128)(2,1)S(1)}, u32[]{:S(2)}, u32[]{:S(2)}) %collective-permute-start.17) | collective-permute-done | bytes 245792 | tf_op jit(solution)/shard_map/ppermute | solution.py:60
  157.1 6.0 %middle.1 = (f32[128,960]{1,0:T(8,128)}, bf16[128,960]{1,0:T(8,128)(2,1)}, bf16[128,960]{1,0:T(8,128)(2,1)}, f32[8,384]{1,0:T(8,128)}) custom-call(s32[40]{0:T(128)} %concatenate.18.ints, bf16[128,960]{1,0:T(8,128)(2,1)} %get-tuple-element.97.d0, bf16[128,960]{1,0:T(8,128)(2,1)} %copy-done.23, bf16[128,960]{1,0:T(8,128)(2,1)} %copy-done.24, ...), custom_call_target="tpu_custom_call" | custom-call | flops 1000 | bytes 1000 | tf_op jit(solution)/shard_map/middle/pallas_call | solution.py:125
  165.9 17.4 %back.1 = (bf16[128,1024]{1,0:T(8,128)(2,1)}, bf16[2048,640]{1,0:T(8,128)(2,1)}) custom-call(s32[40]{0:T(128)} %concatenate.18.ints, bf16[128,1024]{1,0:T(8,128)(2,1)} %get-tuple-element.86.q_ref, bf16[2048,640]{1,0:T(8,128)(2,1)} %get-tuple-element.87.kv_ref, bf16[128,960]{1,0:T(8,128)(2,1)} %get-tuple-element.106.do_ref, ...), custom_call_target="tpu_custom_call" | custom-call | flops 1000 | bytes 1000 | tf_op jit(solution)/shard_map/back/pallas_call | solution.py:125
  183.2 5.3 %convolution_convert_fusion.2 = bf16[960,640]{1,0:T(8,128)(2,1)S(1)} fusion(bf16[2048,960]{1,0:T(8,128)(2,1)S(1)} %copy-done.38, bf16[2048,640]{1,0:T(8,128)(2,1)} %get-tuple-element.132), kind=kOutput, calls=%fused_computation.10 | convolution fusion | flops 2517196800 | bytes 7782400 | tf_op jit(solution)/shard_map/dot_general | solution.py:52
  191.2 4.3 %collective-permute-done.20.its2_ref = bf16[4,120,960]{2,1,0:T(8,128)(2,1)S(1)} collective-permute-done((bf16[4,120,960]{2,1,0:T(8,128)(2,1)S(1)}, bf16[4,120,960]{2,1,0:T(8,128)(2,1)S(1)}, u32[]{:S(2)}, u32[]{:S(2)}) %collective-permute-start.20) | collective-permute-done | bytes 921632 | tf_op jit(solution)/shard_map/ppermute | solution.py:60
  197.1 4.5 %turn.1 = (bf16[120,2560]{1,0:T(8,128)(2,1)}, bf16[120,2560]{1,0:T(8,128)(2,1)}, bf16[120,2560]{1,0:T(8,128)(2,1)}, bf16[120,2560]{1,0:T(8,128)(2,1)}) custom-call(s32[40]{0:T(128)} %concatenate.18.ints, bf16[4,120,1600]{2,1,0:T(8,128)(2,1)} %get-tuple-element.200.mine_ref, bf16[4,120,1600]{2,1,0:T(8,128)(2,1)} %copy-done.6, ...), custom_call_target="tpu_custom_call" | custom-call | flops 1000 | bytes 1000 | tf_op jit(solution)/shard_map/turn/pallas_call | solution.py:125
  203.6 5.5 %all-to-all-start.2 = ((bf16[16,128,640]{2,1,0:T(8,128)(2,1)}), bf16[16,128,640]{2,1,0:T(8,128)(2,1)S(1)}, u32[]{:S(2)}, u32[]{:S(2)}) async-start(bf16[16,128,640]{2,1,0:T(8,128)(2,1)} %bitcast.65), calls=%async_computation.2 | async-start | bytes 5242880 | tf_op jit(solution)/shard_map/all_to_all | solution.py:617
  217.2 9.4 %collective-permute-done.21.refs_1_ = bf16[120,2560]{1,0:T(8,128)(2,1)S(1)} collective-permute-done((bf16[120,2560]{1,0:T(8,128)(2,1)}, bf16[120,2560]{1,0:T(8,128)(2,1)S(1)}, u32[]{:S(2)}, u32[]{:S(2)}) %collective-permute-start.21) | collective-permute-done | bytes 614432 | tf_op jit(solution)/shard_map/ppermute | solution.py:60
  226.6 3.2 %collective-permute-done.22.refs_2_ = bf16[120,2560]{1,0:T(8,128)(2,1)S(1)} collective-permute-done((bf16[120,2560]{1,0:T(8,128)(2,1)}, bf16[120,2560]{1,0:T(8,128)(2,1)S(1)}, u32[]{:S(2)}, u32[]{:S(2)}) %collective-permute-start.22) | collective-permute-done | bytes 614432 | tf_op jit(solution)/shard_map/ppermute | solution.py:60
  229.8 11.9 %collective-permute-done.23.refs_3_ = bf16[120,2560]{1,0:T(8,128)(2,1)S(1)} collective-permute-done((bf16[120,2560]{1,0:T(8,128)(2,1)S(1)}, bf16[120,2560]{1,0:T(8,128)(2,1)S(1)}, u32[]{:S(2)}, u32[]{:S(2)}) %collective-permute-start.23) | collective-permute-done | bytes 614432 | tf_op jit(solution)/shard_map/ppermute | solution.py:60
  242.5 3.1 %columns.1 = (bf16[120,640]{1,0:T(8,128)(2,1)}, bf16[120,640]{1,0:T(8,128)(2,1)}, bf16[120,640]{1,0:T(8,128)(2,1)}, bf16[120,640]{1,0:T(8,128)(2,1)}) custom-call(s32[40]{0:T(128)} %concatenate.18.ints, bf16[120,2560]{1,0:T(8,128)(2,1)} %get-tuple-element.121.refs_0_, bf16[120,2560]{1,0:T(8,128)(2,1)} %copy-done.16, bf16[120,2560]{1,0:T(8,128)(2,1)} %copy-done.17, ...), custom_call_target="tpu_custom_call" | custom-call | flops 1000 | bytes 1000 | tf_op jit(solution)/shard_map/columns/pallas_call | solution.py:125
  247.6 2.6 collective-permute-start.28
  253.2 5.2 %last.1 = bf16[128,960]{1,0:T(8,128)(2,1)} custom-call(s32[40]{0:T(128)} %concatenate.18.ints, bf16[128,1024]{1,0:T(8,128)(2,1)} %get-tuple-element.112.dq_ref, bf16[16,128,640]{2,1,0:T(8,128)(2,1)} %copy-done, bf16[960,1664]{1,0:T(8,128)(2,1)} %get-tuple-element.84.w_ref, bf16[128,960]{1,0:T(8,128)(2,1)} %bitcast.60, f32[1,960]{1,0:T(1,128)} %get-tuple-element.206.gain_ref, ...), custom_call_target="tpu_custom_call" | custom-call | flops 1000 | bytes 1000 | tf_op jit(solution)/shard_map/last/pallas_call | solution.py:125
  260.1 2.7 collective-permute-start.31
  265.0 2.8 collective-permute-start.25
  275.5 2.7 collective-permute-done.26
  280.2 5.5 %all-reduce.5.cloned.1.call-done = (bf16[8,120,640]{2,1,0:T(8,128)(2,1)}, bf16[320,960]{1,0:T(8,128)(2,1)}) async-done(((bf16[8,120,640]{2,1,0:T(8,128)(2,1)}, bf16[320,960]{1,0:T(8,128)(2,1)}), (bf16[8,120,640]{2,1,0:T(8,128)(2,1)}, bf16[320,960]{1,0:T(8,128)(2,1)})) %all-reduce.5.cloned.1.call-update) | async-done | bytes 1843216 | tf_op jit(solution)/shard_map/psum | solution.py:618
  285.7 4.2 %spread.1 = (f32[120,2560]{1,0:T(8,128)}, f32[120,2560]{1,0:T(8,128)}, f32[320,960]{1,0:T(8,128)}, f32[1,120]{1,0:T(1,128)}) custom-call(s32[40]{0:T(128)} %concatenate.18.ints, bf16[8,120,640]{2,1,0:T(8,128)(2,1)} %get-tuple-element.144.g_ref, bf16[320,960]{1,0:T(8,128)(2,1)} %get-tuple-element.196.d_ref, bf16[120,2560]{1,0:T(8,128)(2,1)} %wg_ref.1, ...), custom_call_target="tpu_custom_call" | custom-call | flops 1000 | bytes 1000 | tf_op jit(solution)/shard_map/spread/pallas_call | solution.py:125
  291.3 2.9 finish.1
  (201 shorter events, 83.1 us)
Async XLA Ops:
  7.2 61.4 %all-gather.6.cloned.1.call-start = ((), (), s32[]{:S(2)}) async-start(), calls=%async_computation.4 | async-start | bytes 4456448 | tf_op jit(solution)/shard_map/all_gather | solution.py:570
  9.1 99.8 %all-gather.4.cloned.1.call-start = ((), (), s32[]{:S(2)}) async-start(), calls=%async_computation.3 | async-start | bytes 2359296 | tf_op jit(solution)/shard_map/all_gather | solution.py:577
  14.5 29.6 %collective-permute-start.2 = (bf16[120,2624]{1,0:T(8,128)(2,1)S(1)}, bf16[120,2624]{1,0:T(8,128)(2,1)S(1)}, u32[]{:S(2)}, u32[]{:S(2)}) collective-permute-start(bf16[120,2624]{1,0:T(8,128)(2,1)S(1)} %concatenate.19.refs_0_), channel_id=1, source_target_pairs={{0,2},{2,4},{4,6},{6,0},{1,3},{3,5},{5,7},{7,1},{8,10},{10,12},{12... | collective-permute-start | bytes 1889288 | tf_op jit(solution)/shard_map/ppermute | solution.py:60
  16.5 27.6 %collective-permute-start.1 = (bf16[120,2624]{1,0:T(8,128)(2,1)S(1)}, bf16[120,2624]{1,0:T(8,128)(2,1)S(1)}, u32[]{:S(2)}, u32[]{:S(2)}) collective-permute-start(bf16[120,2624]{1,0:T(8,128)(2,1)S(1)} %concatenate.19.refs_0_), channel_id=1, source_target_pairs={{0,4},{2,6},{4,0},{6,2},{1,5},{3,7},{5,1},{7,3},{8,12},{10,14},{12... | collective-permute-start | bytes 1889288 | tf_op jit(solution)/shard_map/ppermute | solution.py:60
  17.6 29.9 %collective-permute-start = (bf16[120,2624]{1,0:T(8,128)(2,1)S(1)}, bf16[120,2624]{1,0:T(8,128)(2,1)}, u32[]{:S(2)}, u32[]{:S(2)}) collective-permute-start(bf16[120,2624]{1,0:T(8,128)(2,1)S(1)} %concatenate.19.refs_0_), channel_id=1, source_target_pairs={{0,6},{2,0},{4,2},{6,4},{1,7},{3,1},{5,3},{7,5},{8,14},{10,8},{12,... | collective-permute-start | bytes 1889288 | tf_op jit(solution)/shard_map/ppermute | solution.py:60
  20.2 29.1 %collective-permute-start.3 = (bf16[120,2624]{1,0:T(8,128)(2,1)S(1)}, bf16[120,2624]{1,0:T(8,128)(2,1)}, u32[]{:S(2)}, u32[]{:S(2)}) collective-permute-start(bf16[120,2624]{1,0:T(8,128)(2,1)S(1)} %concatenate.19.refs_0_), channel_id=1, source_target_pairs={{0,1},{1,0},{2,3},{3,2},{4,5},{5,4},{6,7},{7,6},{8,9},{9,8},{10,11... | collective-permute-start | bytes 1889288 | tf_op jit(solution)/shard_map/ppermute | solution.py:60
  57.9 49.5 %all-to-all-start = ((bf16[8,120,640]{2,1,0:T(8,128)(2,1)}), bf16[8,120,640]{2,1,0:T(8,128)(2,1)S(1)}, u32[]{:S(2)}, u32[]{:S(2)}) async-start(bf16[8,120,640]{2,1,0:T(8,128)(2,1)} %copy.106), calls=%async_computation | async-start | bytes 2457600 | tf_op jit(solution)/shard_map/all_to_all | solution.py:586
  91.2 9.4 %collective-permute-start.9 = (bf16[128,960]{1,0:T(8,128)(2,1)}, bf16[128,960]{1,0:T(8,128)(2,1)S(1)}, u32[]{:S(2)}, u32[]{:S(2)}) collective-permute-start(bf16[128,960]{1,0:T(8,128)(2,1)} %get-tuple-element.91.refs_0_), channel_id=1, source_target_pairs={{0,2},{2,4},{4,6},{6,0},{1,3},{3,5},{5,7},{7,1},{8,10},{10,12},{12... | collective-permute-start | bytes 737288 | tf_op jit(solution)/shard_map/ppermute | solution.py:60
  92.7 10.9 %collective-permute-start.8 = (bf16[128,960]{1,0:T(8,128)(2,1)}, bf16[128,960]{1,0:T(8,128)(2,1)S(1)}, u32[]{:S(2)}, u32[]{:S(2)}) collective-permute-start(bf16[128,960]{1,0:T(8,128)(2,1)} %get-tuple-element.91.refs_0_), channel_id=1, source_target_pairs={{0,4},{2,6},{4,0},{6,2},{1,5},{3,7},{5,1},{7,3},{8,12},{10,14},{12... | collective-permute-start | bytes 737288 | tf_op jit(solution)/shard_map/ppermute | solution.py:60
  93.3 13.9 %collective-permute-start.7 = (bf16[128,960]{1,0:T(8,128)(2,1)}, bf16[128,960]{1,0:T(8,128)(2,1)S(1)}, u32[]{:S(2)}, u32[]{:S(2)}) collective-permute-start(bf16[128,960]{1,0:T(8,128)(2,1)} %get-tuple-element.91.refs_0_), channel_id=1, source_target_pairs={{0,6},{2,0},{4,2},{6,4},{1,7},{3,1},{5,3},{7,5},{8,14},{10,8},{12,... | collective-permute-start | bytes 737288 | tf_op jit(solution)/shard_map/ppermute | solution.py:60
  95.8 13.0 %collective-permute-start.10 = (bf16[128,960]{1,0:T(8,128)(2,1)}, bf16[128,960]{1,0:T(8,128)(2,1)S(1)}, u32[]{:S(2)}, u32[]{:S(2)}) collective-permute-start(bf16[128,960]{1,0:T(8,128)(2,1)} %get-tuple-element.91.refs_0_), channel_id=1, source_target_pairs={{0,1},{1,0},{2,3},{3,2},{4,5},{5,4},{6,7},{7,6},{8,9},{9,8},{10,11... | collective-permute-start | bytes 737288 | tf_op jit(solution)/shard_map/ppermute | solution.py:60
  100.6 8.3 %collective-permute-start.13 = (bf16[128,960]{1,0:T(8,128)(2,1)S(1)}, bf16[128,960]{1,0:T(8,128)(2,1)S(1)}, u32[]{:S(2)}, u32[]{:S(2)}) collective-permute-start(bf16[128,960]{1,0:T(8,128)(2,1)S(1)} %collective-permute-done.9.refs_3_), channel_id=1, source_target_pairs={{0,1},{1,0},{2,3},{3,2},{4,5},{5,4},{6,7},{7,6},{8,9},{9,8},{10,11... | collective-permute-start | bytes 737288 | tf_op jit(solution)/shard_map/ppermute | solution.py:60
  124.5 21.8 %all-to-all-start.1 = ((bf16[8,120,640]{2,1,0:T(8,128)(2,1)}), bf16[8,120,640]{2,1,0:T(8,128)(2,1)S(1)}, u32[]{:S(2)}, u32[]{:S(2)}) async-start(bf16[8,120,640]{2,1,0:T(8,128)(2,1)} %get-tuple-element.101), calls=%async_computation.1 | async-start | bytes 2457600 | tf_op jit(solution)/shard_map/all_to_all | solution.py:597
  129.3 74.3 %all-reduce.7.cloned.1.call-start = ((), (), s32[]{:S(2)}) async-start(), calls=%async_computation.6 | async-start | bytes 3768320 | tf_op jit(solution)/shard_map/psum | solution.py:609
  132.9 17.0 %collective-permute-start.15 = (bf16[128,960]{1,0:T(8,128)(2,1)}, bf16[128,960]{1,0:T(8,128)(2,1)S(1)}, u32[]{:S(2)}, u32[]{:S(2)}) collective-permute-start(bf16[128,960]{1,0:T(8,128)(2,1)} %get-tuple-element.98), channel_id=1, source_target_pairs={{0,2},{2,4},{4,6},{6,0},{1,3},{3,5},{5,7},{7,1},{8,10},{10,12},{12... | collective-permute-start | bytes 737288 | tf_op jit(solution)/shard_map/ppermute | solution.py:60
  134.3 17.5 %collective-permute-start.16 = (bf16[128,960]{1,0:T(8,128)(2,1)}, bf16[128,960]{1,0:T(8,128)(2,1)S(1)}, u32[]{:S(2)}, u32[]{:S(2)}) collective-permute-start(bf16[128,960]{1,0:T(8,128)(2,1)} %get-tuple-element.99), channel_id=1, source_target_pairs={{0,4},{2,6},{4,0},{6,2},{1,5},{3,7},{5,1},{7,3},{8,12},{10,14},{12... | collective-permute-start | bytes 737288 | tf_op jit(solution)/shard_map/ppermute | solution.py:60
  135.0 21.4 %collective-permute-start.17 = (bf16[128,960]{1,0:T(8,128)(2,1)}, bf16[128,960]{1,0:T(8,128)(2,1)S(1)}, u32[]{:S(2)}, u32[]{:S(2)}) collective-permute-start(bf16[128,960]{1,0:T(8,128)(2,1)} %get-tuple-element.100), channel_id=1, source_target_pairs={{0,6},{2,0},{4,2},{6,4},{1,7},{3,1},{5,3},{7,5},{8,14},{10,8},{12,... | collective-permute-start | bytes 737288 | tf_op jit(solution)/shard_map/ppermute | solution.py:60
  203.6 48.1 %all-to-all-start.2 = ((bf16[16,128,640]{2,1,0:T(8,128)(2,1)}), bf16[16,128,640]{2,1,0:T(8,128)(2,1)S(1)}, u32[]{:S(2)}, u32[]{:S(2)}) async-start(bf16[16,128,640]{2,1,0:T(8,128)(2,1)} %bitcast.65), calls=%async_computation.2 | async-start | bytes 5242880 | tf_op jit(solution)/shard_map/all_to_all | solution.py:617
  209.0 76.7 %all-reduce.5.cloned.1.call-start = ((), (), s32[]{:S(2)}) async-start(), calls=%async_computation.5 | async-start | bytes 3768320 | tf_op jit(solution)/shard_map/psum | solution.py:618
  209.6 17.0 %collective-permute-start.21 = (bf16[120,2560]{1,0:T(8,128)(2,1)}, bf16[120,2560]{1,0:T(8,128)(2,1)S(1)}, u32[]{:S(2)}, u32[]{:S(2)}) collective-permute-start(bf16[120,2560]{1,0:T(8,128)(2,1)} %get-tuple-element.122), channel_id=1, source_target_pairs={{0,2},{2,4},{4,6},{6,0},{1,3},{3,5},{5,7},{7,1},{8,10},{10,12},{12... | collective-permute-start | bytes 1843208 | tf_op jit(solution)/shard_map/ppermute | solution.py:60
  211.2 18.5 %collective-permute-start.22 = (bf16[120,2560]{1,0:T(8,128)(2,1)}, bf16[120,2560]{1,0:T(8,128)(2,1)S(1)}, u32[]{:S(2)}, u32[]{:S(2)}) collective-permute-start(bf16[120,2560]{1,0:T(8,128)(2,1)} %get-tuple-element.123), channel_id=1, source_target_pairs={{0,4},{2,6},{4,0},{6,2},{1,5},{3,7},{5,1},{7,3},{8,12},{10,14},{12... | collective-permute-start | bytes 1843208 | tf_op jit(solution)/shard_map/ppermute | solution.py:60
  213.7 28.0 %collective-permute-start.23 = (bf16[120,2560]{1,0:T(8,128)(2,1)S(1)}, bf16[120,2560]{1,0:T(8,128)(2,1)S(1)}, u32[]{:S(2)}, u32[]{:S(2)}) collective-permute-start(bf16[120,2560]{1,0:T(8,128)(2,1)S(1)} %copy-done.42), channel_id=1, source_target_pairs={{0,6},{2,0},{4,2},{6,4},{1,7},{3,1},{5,3},{7,5},{8,14},{10,8},{12,... | collective-permute-start | bytes 1843208 | tf_op jit(solution)/shard_map/ppermute | solution.py:60
  245.7 12.8 %collective-permute-start.27 = (bf16[120,640]{1,0:T(8,128)(2,1)}, bf16[120,640]{1,0:T(8,128)(2,1)S(1)}, u32[]{:S(2)}, u32[]{:S(2)}) collective-permute-start(bf16[120,640]{1,0:T(8,128)(2,1)} %get-tuple-element.136), channel_id=1, source_target_pairs={{0,32},{32,64},{64,96},{96,0},{1,33},{33,65},{65,97},{97,1},{2,34}... | collective-permute-start | bytes 460808 | tf_op jit(solution)/shard_map/ppermute | solution.py:60
  247.6 10.8 %collective-permute-start.28 = (bf16[120,640]{1,0:T(8,128)(2,1)}, bf16[120,640]{1,0:T(8,128)(2,1)S(1)}, u32[]{:S(2)}, u32[]{:S(2)}) collective-permute-start(bf16[120,640]{1,0:T(8,128)(2,1)} %get-tuple-element.137), channel_id=1, source_target_pairs={{0,64},{32,96},{64,0},{96,32},{1,65},{33,97},{65,1},{97,33},{2,66}... | collective-permute-start | bytes 460808 | tf_op jit(solution)/shard_map/ppermute | solution.py:60
  258.5 9.3 %collective-permute-start.32 = (bf16[120,640]{1,0:T(8,128)(2,1)S(1)}, bf16[120,640]{1,0:T(8,128)(2,1)S(1)}, u32[]{:S(2)}, u32[]{:S(2)}) collective-permute-start(bf16[120,640]{1,0:T(8,128)(2,1)S(1)} %add_convert_fusion.2), channel_id=1, source_target_pairs={{0,8},{8,16},{16,24},{24,0},{1,9},{9,17},{17,25},{25,1},{2,10},{10... | collective-permute-start | bytes 460808 | tf_op jit(solution)/shard_map/ppermute | solution.py:60
  260.1 9.5 %collective-permute-start.31 = (bf16[120,640]{1,0:T(8,128)(2,1)S(1)}, bf16[120,640]{1,0:T(8,128)(2,1)S(1)}, u32[]{:S(2)}, u32[]{:S(2)}) collective-permute-start(bf16[120,640]{1,0:T(8,128)(2,1)S(1)} %add_convert_fusion.2), channel_id=1, source_target_pairs={{0,16},{8,24},{16,0},{24,8},{1,17},{9,25},{17,1},{25,9},{2,18},{10... | collective-permute-start | bytes 460808 | tf_op jit(solution)/shard_map/ppermute | solution.py:60
  264.2 9.4 %collective-permute-start.24 = (bf16[128,960]{1,0:T(8,128)(2,1)S(1)}, bf16[128,960]{1,0:T(8,128)(2,1)S(1)}, u32[]{:S(2)}, u32[]{:S(2)}) collective-permute-start(bf16[128,960]{1,0:T(8,128)(2,1)S(1)} %copy-done.45), channel_id=1, source_target_pairs={{0,2},{2,4},{4,6},{6,0},{1,3},{3,5},{5,7},{7,1},{8,10},{10,12},{12... | collective-permute-start | bytes 737288 | tf_op jit(solution)/shard_map/ppermute | solution.py:60
  265.0 10.5 %collective-permute-start.25 = (bf16[128,960]{1,0:T(8,128)(2,1)S(1)}, bf16[128,960]{1,0:T(8,128)(2,1)S(1)}, u32[]{:S(2)}, u32[]{:S(2)}) collective-permute-start(bf16[128,960]{1,0:T(8,128)(2,1)S(1)} %copy-done.44), channel_id=1, source_target_pairs={{0,4},{2,6},{4,0},{6,2},{1,5},{3,7},{5,1},{7,3},{8,12},{10,14},{12... | collective-permute-start | bytes 737288 | tf_op jit(solution)/shard_map/ppermute | solution.py:60
  267.8 10.4 %collective-permute-start.26 = (bf16[128,960]{1,0:T(8,128)(2,1)S(1)}, bf16[128,960]{1,0:T(8,128)(2,1)S(1)}, u32[]{:S(2)}, u32[]{:S(2)}) collective-permute-start(bf16[128,960]{1,0:T(8,128)(2,1)S(1)} %copy-done.43), channel_id=1, source_target_pairs={{0,6},{2,0},{4,2},{6,4},{1,7},{3,1},{5,3},{7,5},{8,14},{10,8},{12,... | collective-permute-start | bytes 737288 | tf_op jit(solution)/shard_map/ppermute | solution.py:60
  270.0 19.9 %collective-permute-start.35 = (bf16[120,640]{1,0:T(8,128)(2,1)S(1)}, bf16[120,640]{1,0:T(8,128)(2,1)S(1)}, u32[]{:S(2)}, u32[]{:S(2)}) collective-permute-start(bf16[120,640]{1,0:T(8,128)(2,1)S(1)} %add_convert_fusion.1.p0), channel_id=1, source_target_pairs={{0,32},{32,64},{64,96},{96,0},{1,33},{33,65},{65,97},{97,1},{2,34}... | collective-permute-start | bytes 460808 | tf_op jit(solution)/shard_map/ppermute | solution.py:60
  270.3 19.6 %collective-permute-start.34 = (bf16[120,640]{1,0:T(8,128)(2,1)S(1)}, bf16[120,640]{1,0:T(8,128)(2,1)S(1)}, u32[]{:S(2)}, u32[]{:S(2)}) collective-permute-start(bf16[120,640]{1,0:T(8,128)(2,1)S(1)} %add_convert_fusion.1.p0), channel_id=1, source_target_pairs={{0,64},{32,96},{64,0},{96,32},{1,65},{33,97},{65,1},{97,33},{2,66}... | collective-permute-start | bytes 460808 | tf_op jit(solution)/shard_map/ppermute | solution.py:60
  273.6 16.3 %collective-permute-start.33 = (bf16[120,640]{1,0:T(8,128)(2,1)S(1)}, bf16[120,640]{1,0:T(8,128)(2,1)S(1)}, u32[]{:S(2)}, u32[]{:S(2)}) collective-permute-start(bf16[120,640]{1,0:T(8,128)(2,1)S(1)} %add_convert_fusion.1.p0), channel_id=1, source_target_pairs={{0,96},{32,0},{64,32},{96,64},{1,97},{33,1},{65,33},{97,65},{2,98}... | collective-permute-start | bytes 460808 | tf_op jit(solution)/shard_map/ppermute | solution.py:60
  (57 other events, 635.2 us)
Sparse Core Ops, SparseCore 0:
  10.7 53.4 all-gather.5
  65.9 25.2 all-gather.3
  147.5 56.0 all-reduce.6
  212.1 73.5 all-reduce.4
